TPU v7x, 32 devices: a whole 2x2x4 slice. The times are simulated.
32 devices in a mesh: section: 2 (over x), dp: 16 (over z, y, core).
Axes of the slice: x: 2, y: 2, z: 4, core: 2. Of those that a mesh axis runs over, the one named last changes fastest.
Arguments:
- text: bfloat16 [4096, 768], P('dp', 'section'), may hold values from -6 to 6
- image: bfloat16 [64, 576, 768], P('dp', 'section'), may hold values from -6 to 6
- lengths: int32 [64], P('dp'), may hold values from 5 to 64
- self_gain: bfloat16 [2, 768], P('section', 'dp'), may hold values from 0.25 to 1.75
- self_shift: bfloat16 [2, 768], P('section', 'dp'), may hold values from -1.75 to 1.75
- heads_in: bfloat16 [2, 768, 2304], P('section', 'dp'), may hold values from -0.3125 to 0.3125
- heads_out: bfloat16 [2, 768, 768], P('section', 'dp'), may hold values from -0.21875 to 0.21875
- feed_gain: bfloat16 [2, 768], P('section', 'dp'), may hold values from 0.25 to 1.75
- feed_shift: bfloat16 [2, 768], P('section', 'dp'), may hold values from -1.75 to 1.75
- up_weight: bfloat16 [2, 768, 3072], P('section', 'dp'), may hold values from -0.21875 to 0.21875
- up_bias: bfloat16 [2, 3072], P('section', 'dp'), may hold values from -1.75 to 1.75
- down_weight: bfloat16 [2, 3072, 768], P('section', 'dp'), may hold values from -0.109375 to 0.109375
- down_bias: bfloat16 [2, 768], P('section', 'dp'), may hold values from -1.75 to 1.75
- cross_gain: bfloat16 [768], P(('section', 'dp')), may hold values from 0.25 to 1.75
- cross_shift: bfloat16 [768], P(('section', 'dp')), may hold values from -1.75 to 1.75
- cross_query: bfloat16 [768, 768], P(('section', 'dp')), may hold values from -0.3125 to 0.3125
- cross_keys: bfloat16 [768, 1536], P(('section', 'dp')), may hold values from -0.21875 to 0.21875
- cross_out: bfloat16 [768, 768], P(('section', 'dp')), may hold values from -0.4375 to 0.4375
- cotangent: bfloat16 [4096, 768], P('dp', 'section'), may hold values from -6 to 6
Outputs:
- layer_out: float32 [4096, 768], P('dp', 'section')
- text_grad: float32 [4096, 768], P('dp', 'section')
- image_grad: float32 [64, 576, 768], P('dp', 'section')
- self_gain_grad: float32 [2, 768], P('section', 'dp')
- self_shift_grad: float32 [2, 768], P('section', 'dp')
- heads_in_grad: float32 [2, 768, 2304], P('section', 'dp')
- heads_out_grad: float32 [2, 768, 768], P('section', 'dp')
- feed_gain_grad: float32 [2, 768], P('section', 'dp')
- feed_shift_grad: float32 [2, 768], P('section', 'dp')
- up_weight_grad: float32 [2, 768, 3072], P('section', 'dp')
- up_bias_grad: float32 [2, 3072], P('section', 'dp')
- down_weight_grad: float32 [2, 3072, 768], P('section', 'dp')
- down_bias_grad: float32 [2, 768], P('section', 'dp')
- cross_gain_grad: float32 [768], P(('section', 'dp'))
- cross_shift_grad: float32 [768], P(('section', 'dp'))
- cross_query_grad: float32 [768, 768], P(('section', 'dp'))
- cross_keys_grad: float32 [768, 1536], P(('section', 'dp'))
- cross_out_grad: float32 [768, 768], P(('section', 'dp'))
Inputs may be any that keep to these rules, and one draw needn't show every extreme that they name: `lengths`: a caption of length n holds its tokens in its first n of 64 slots; the rest is padding.
All inputs are finite; a program needn't handle non-finite values.
Results may differ from a plain program's by a relative error of at most 0.025.
Values may be sent and summed in bfloat16 or wider, within the bound.
No kernel may reach another device: no remote copies, remote signals or barrier semaphores. Data moves between devices by JAX's collectives and lax.ppermute only.
A program may use at most 320 MiB of HBM per device.

v0:
```python
import jax
import jax.numpy as jnp
from jax import lax
from jax.sharding import PartitionSpec as P

HEADS = 12
HEAD_DIM = 64
MICRO = 2


EPS = 1e-05
MASKED = -1000000000.0


def from_behind(value, axis, steps):
    count = lax.axis_size(axis)
    leading, last = (max(0, -steps), min(count, count - steps))
    return lax.ppermute(value, axis, [(source, source + steps) for source in range(leading, last)])


def norm(values, gain, shift):
    centred = values - jnp.mean(values, -1, keepdims=True)
    spread = jnp.mean(centred * centred, -1, keepdims=True)
    return centred * lax.rsqrt(spread + EPS) * gain + shift


def softmax_rows(scores):
    top = jnp.max(scores, -1, keepdims=True)
    raised = jnp.exp(scores - top)
    return raised / jnp.sum(raised, -1, keepdims=True)


def gelu_exact(values):
    return jax.nn.gelu(values, approximate=False)


def product(left, right):
    return jnp.dot(left, right, preferred_element_type=jnp.float32)


def weight_grad(left, right):
    return lax.dot_general(
        left, right, (((0,), (0,)), ((), ())), preferred_element_type=jnp.float32
    )


def input_grad(grad, weight):
    return lax.dot_general(
        grad, weight, (((1,), (1,)), ((), ())), preferred_element_type=jnp.float32
    )


def attend(queries, keys, values, keep):
    scores = jnp.einsum(
        "cqhd,ckhd->chqk", queries, keys, preferred_element_type=jnp.float32
    ) * HEAD_DIM ** (-0.5)
    if keep is not None:
        scores = jnp.where(keep, scores, MASKED)
    chances = softmax_rows(scores)
    chances_low = chances.astype(jnp.bfloat16)
    mixed = jnp.einsum("chqk,ckhd->cqhd", chances_low, values, preferred_element_type=jnp.float32)
    return (chances, chances_low, mixed)


def attend_back(queries, keys, values, chances, chances_low, grad_mixed):
    grad_chances = jnp.einsum(
        "cqhd,ckhd->chqk", grad_mixed, values, preferred_element_type=jnp.float32
    )
    grad_scores = chances * (grad_chances - jnp.sum(grad_chances * chances, -1, keepdims=True))
    grad_low = grad_scores.astype(jnp.bfloat16)
    scale = HEAD_DIM ** (-0.5)
    query_part = (
        jnp.einsum("chqk,ckhd->cqhd", grad_low, keys, preferred_element_type=jnp.float32) * scale
    )
    key_part = (
        jnp.einsum("chqk,cqhd->ckhd", grad_low, queries, preferred_element_type=jnp.float32) * scale
    )
    value_part = jnp.einsum(
        "chqk,cqhd->ckhd", chances_low, grad_mixed, preferred_element_type=jnp.float32
    )
    return (query_part, key_part, value_part)


def run_layer(inputs, keep, weights, cross_weights, pair_source, later, image_rows):
    (
        self_gain,
        self_shift,
        heads_in,
        heads_out,
        feed_gain,
        feed_shift,
        up_weight,
        up_bias,
        down_weight,
        down_bias,
    ) = weights
    cross_gain, cross_shift, cross_query, cross_keys, cross_out = cross_weights
    rows, width = inputs.shape
    captions = keep.shape[0]
    slots = rows // captions
    normed = norm(inputs, self_gain.astype(jnp.float32), self_shift.astype(jnp.float32)).astype(
        jnp.bfloat16
    )
    projected = (
        product(normed, heads_in).astype(jnp.bfloat16).reshape(captions, slots, 3, HEADS, HEAD_DIM)
    )
    queries, keys, values = (projected[:, :, 0], projected[:, :, 1], projected[:, :, 2])
    chances, chances_low, mixed = attend(queries, keys, values, keep)
    mixed_low = mixed.reshape(rows, width).astype(jnp.bfloat16)
    first_out = inputs + product(mixed_low, heads_out)

    def with_cross():
        pairs = pair_source()
        cross_normed = norm(
            first_out, cross_gain.astype(jnp.float32), cross_shift.astype(jnp.float32)
        ).astype(jnp.bfloat16)
        cross_queries = (
            product(cross_normed, cross_query)
            .astype(jnp.bfloat16)
            .reshape(captions, slots, HEADS, HEAD_DIM)
        )
        split = pairs.reshape(captions, image_rows, 2, HEADS, HEAD_DIM)
        cross_chances, cross_low, cross_mixed = attend(
            cross_queries, split[:, :, 0], split[:, :, 1], None
        )
        cross_mixed_low = cross_mixed.reshape(rows, width).astype(jnp.bfloat16)
        middle = first_out + product(cross_mixed_low, cross_out)
        return (
            middle,
            (cross_normed, cross_queries, cross_chances, cross_low, cross_mixed_low, pairs),
        )

    def without_cross():
        return (
            first_out,
            (
                jnp.zeros((rows, width), jnp.bfloat16),
                jnp.zeros((captions, slots, HEADS, HEAD_DIM), jnp.bfloat16),
                jnp.zeros((captions, HEADS, slots, image_rows), jnp.float32),
                jnp.zeros((captions, HEADS, slots, image_rows), jnp.bfloat16),
                jnp.zeros((rows, width), jnp.bfloat16),
                jnp.zeros((captions, image_rows, 2 * width), jnp.bfloat16),
            ),
        )

    middle, cross_saved = lax.cond(later, with_cross, without_cross)
    feed_normed = norm(
        middle, feed_gain.astype(jnp.float32), feed_shift.astype(jnp.float32)
    ).astype(jnp.bfloat16)
    raised = product(feed_normed, up_weight) + up_bias.astype(jnp.float32)
    active = gelu_exact(raised).astype(jnp.bfloat16)
    result = middle + product(active, down_weight) + down_bias.astype(jnp.float32)
    saved = (
        normed,
        queries,
        keys,
        values,
        chances,
        chances_low,
        mixed_low,
        first_out,
        middle,
        cross_saved,
        feed_normed,
        raised,
        active,
    )
    return (result, saved)


def layer_backward(inputs, keep, weights, cross_weights, pair_source, later, image_rows, grad_out):
    (
        self_gain,
        self_shift,
        heads_in,
        heads_out,
        feed_gain,
        feed_shift,
        up_weight,
        up_bias,
        down_weight,
        down_bias,
    ) = weights
    cross_gain, cross_shift, cross_query, cross_keys, cross_out = cross_weights
    rows, width = inputs.shape
    captions = keep.shape[0]
    slots = rows // captions
    result, saved = run_layer(inputs, keep, weights, cross_weights, pair_source, later, image_rows)
    (
        normed,
        queries,
        keys,
        values,
        chances,
        chances_low,
        mixed_low,
        first_out,
        middle,
        cross_saved,
        feed_normed,
        raised,
        active,
    ) = saved
    grad_low = grad_out.astype(jnp.bfloat16)
    down_term = weight_grad(active, grad_low)
    down_bias_term = jnp.sum(grad_out, 0)
    grad_active = input_grad(grad_low, down_weight)
    _, gelu_back = jax.vjp(gelu_exact, raised)
    grad_raised = gelu_back(grad_active)[0].astype(jnp.bfloat16)
    up_term = weight_grad(feed_normed, grad_raised)
    up_bias_term = jnp.sum(grad_raised.astype(jnp.float32), 0)
    _, feed_back = jax.vjp(
        norm, middle, feed_gain.astype(jnp.float32), feed_shift.astype(jnp.float32)
    )
    grad_middle, feed_gain_term, feed_shift_term = feed_back(input_grad(grad_raised, up_weight))
    grad_middle = grad_middle + grad_out

    def cross_back():
        cross_normed, cross_queries, cross_chances, cross_low, cross_mixed_low, pairs = cross_saved
        split = pairs.reshape(captions, image_rows, 2, HEADS, HEAD_DIM)
        branch_low = grad_middle.astype(jnp.bfloat16)
        out_term = weight_grad(cross_mixed_low, branch_low)
        grad_mixed = (
            input_grad(branch_low, cross_out)
            .astype(jnp.bfloat16)
            .reshape(captions, slots, HEADS, HEAD_DIM)
        )
        query_part, key_part, value_part = attend_back(
            cross_queries, split[:, :, 0], split[:, :, 1], cross_chances, cross_low, grad_mixed
        )
        grad_queries = query_part.reshape(rows, width).astype(jnp.bfloat16)
        grad_pairs = (
            jnp.stack([key_part, value_part], 2)
            .reshape(captions, image_rows, 2 * width)
            .astype(jnp.bfloat16)
        )
        query_term = weight_grad(cross_normed, grad_queries)
        _, cross_norm_back = jax.vjp(
            norm, first_out, cross_gain.astype(jnp.float32), cross_shift.astype(jnp.float32)
        )
        grad_first, gain_term, shift_term = cross_norm_back(input_grad(grad_queries, cross_query))
        return (grad_first + grad_middle, (gain_term, shift_term, query_term, out_term), grad_pairs)

    def skip_back():
        empty_terms = (
            jnp.zeros((width,), jnp.float32),
            jnp.zeros((width,), jnp.float32),
            jnp.zeros((width, width), jnp.float32),
            jnp.zeros((width, width), jnp.float32),
        )
        return (
            grad_middle,
            empty_terms,
            jnp.zeros((captions, image_rows, 2 * width), jnp.bfloat16),
        )

    grad_first, cross_terms, grad_pairs = lax.cond(later, cross_back, skip_back)
    branch_low = grad_first.astype(jnp.bfloat16)
    heads_out_term = weight_grad(mixed_low, branch_low)
    grad_mixed = (
        input_grad(branch_low, heads_out)
        .astype(jnp.bfloat16)
        .reshape(captions, slots, HEADS, HEAD_DIM)
    )
    query_part, key_part, value_part = attend_back(
        queries, keys, values, chances, chances_low, grad_mixed
    )
    grad_projected = (
        jnp.stack([query_part, key_part, value_part], 2)
        .reshape(rows, 3 * width)
        .astype(jnp.bfloat16)
    )
    heads_in_term = weight_grad(normed, grad_projected)
    _, self_back = jax.vjp(
        norm, inputs, self_gain.astype(jnp.float32), self_shift.astype(jnp.float32)
    )
    grad_inputs, self_gain_term, self_shift_term = self_back(input_grad(grad_projected, heads_in))
    grad_inputs = grad_inputs + grad_first
    section_terms = (
        self_gain_term,
        self_shift_term,
        heads_in_term,
        heads_out_term,
        feed_gain_term,
        feed_shift_term,
        up_term,
        up_bias_term,
        down_term,
        down_bias_term,
    )
    return (grad_inputs, section_terms, cross_terms, grad_pairs)


def body(
    text,
    image,
    lengths,
    self_gain,
    self_shift,
    heads_in,
    heads_out,
    feed_gain,
    feed_shift,
    up_weight,
    up_bias,
    down_weight,
    down_bias,
    cross_gain,
    cross_shift,
    cross_query,
    cross_keys,
    cross_out,
    cotangent,
):
    section = lax.axis_index("section")
    first = section == 0
    later = section == 1
    micro = MICRO
    captions = image.shape[0] // micro
    slots = text.shape[0] // image.shape[0]
    rows = captions * slots
    half_image = image.shape[1]
    width = image.shape[2]
    image_rows = 2 * half_image
    whole = lax.all_to_all(
        jnp.stack([text, cotangent]), "section", split_axis=0, concat_axis=2, tiled=True
    )[0]
    section_parts = (
        lax.all_gather(self_gain, "dp", axis=1, tiled=True),
        lax.all_gather(self_shift, "dp", axis=1, tiled=True),
        lax.all_gather(heads_in, "dp", axis=1, tiled=True),
        lax.all_gather(heads_out, "dp", axis=1, tiled=True),
        lax.all_gather(feed_gain, "dp", axis=1, tiled=True),
        lax.all_gather(feed_shift, "dp", axis=1, tiled=True),
        lax.all_gather(up_weight, "dp", axis=1, tiled=True),
        lax.all_gather(up_bias, "dp", axis=1, tiled=True),
        lax.all_gather(down_weight, "dp", axis=1, tiled=True),
        lax.all_gather(down_bias, "dp", axis=1, tiled=True),
    )
    weights = tuple((part[0] for part in section_parts))
    cross_weights = (
        lax.all_gather(cross_gain, ("section", "dp"), axis=0, tiled=True),
        lax.all_gather(cross_shift, ("section", "dp"), axis=0, tiled=True),
        lax.all_gather(cross_query, ("section", "dp"), axis=0, tiled=True),
        lax.all_gather(cross_keys, ("section", "dp"), axis=0, tiled=True),
        lax.all_gather(cross_out, ("section", "dp"), axis=0, tiled=True),
    )
    place = jnp.arange(slots)
    causal = (place[None, :] <= place[:, None])[None, :, :]

    def mask_for(index):
        caption_lengths = lax.dynamic_slice_in_dim(lengths, index * captions, captions)
        filled = place[None, None, :] < caption_lengths[:, None, None]
        return (causal & filled)[:, None, :, :]

    received_rows = jnp.zeros((rows, width), jnp.bfloat16)
    received_extra = jnp.zeros((captions, half_image, width), jnp.bfloat16)
    outputs = jnp.zeros((micro * rows, width), jnp.float32)
    kept_rows = []
    kept_pairs = []
    for moment in range(micro + 1):
        index = jnp.clip(moment - section, 0, micro - 1)
        keep = mask_for(index)
        own_image = lax.dynamic_slice_in_dim(image, index * captions, captions)
        given = lax.dynamic_slice_in_dim(whole, index * rows, rows).astype(jnp.float32)
        inputs = jnp.where(first, given, received_rows.astype(jnp.float32))
        cross_keys_full = cross_weights[3]
        arrived = received_extra

        def pair_source():
            both = jnp.concatenate([arrived, own_image], 1)
            return (
                product(both.reshape(captions * image_rows, width), cross_keys_full)
                .astype(jnp.bfloat16)
                .reshape(captions, image_rows, 2 * width)
            )

        result, saved = run_layer(
            inputs, keep, weights, cross_weights, pair_source, later, image_rows
        )
        kept_rows.append(received_rows)
        kept_pairs.append(saved[9][5])
        if moment >= 1:
            outputs = jnp.where(
                later, lax.dynamic_update_slice_in_dim(outputs, result, index * rows, 0), outputs
            )
        if moment < micro:
            received_rows, received_extra = from_behind(
                (result.astype(jnp.bfloat16), own_image), "section", 1
            )
    section_parts = (
        lax.all_gather(self_gain, "dp", axis=1, tiled=True),
        lax.all_gather(self_shift, "dp", axis=1, tiled=True),
        lax.all_gather(heads_in, "dp", axis=1, tiled=True),
        lax.all_gather(heads_out, "dp", axis=1, tiled=True),
        lax.all_gather(feed_gain, "dp", axis=1, tiled=True),
        lax.all_gather(feed_shift, "dp", axis=1, tiled=True),
        lax.all_gather(up_weight, "dp", axis=1, tiled=True),
        lax.all_gather(up_bias, "dp", axis=1, tiled=True),
        lax.all_gather(down_weight, "dp", axis=1, tiled=True),
        lax.all_gather(down_bias, "dp", axis=1, tiled=True),
    )
    weights = tuple((part[0] for part in section_parts))
    cross_weights = (
        lax.all_gather(cross_gain, ("section", "dp"), axis=0, tiled=True),
        lax.all_gather(cross_shift, ("section", "dp"), axis=0, tiled=True),
        lax.all_gather(cross_query, ("section", "dp"), axis=0, tiled=True),
        lax.all_gather(cross_keys, ("section", "dp"), axis=0, tiled=True),
        lax.all_gather(cross_out, ("section", "dp"), axis=0, tiled=True),
    )
    cross_keys_full = cross_weights[3]
    stored_rows = jnp.stack(kept_rows[1:])
    stored_pairs = jnp.stack(kept_pairs[1:])
    received_grad = jnp.zeros((rows, width), jnp.bfloat16)
    received_pair_grad = jnp.zeros((captions, half_image, 2 * width), jnp.bfloat16)
    text_grads = jnp.zeros((micro * rows, width), jnp.float32)
    image_grads = jnp.zeros(image.shape, jnp.float32)
    section_sums = tuple((jnp.zeros(part.shape, jnp.float32) for part in weights))
    cross_sums = tuple((jnp.zeros(part.shape, jnp.float32) for part in cross_weights))
    for moment in range(micro + 1):
        position = moment - 1 + section
        index = jnp.clip(position, 0, micro - 1)
        valid = (position >= 0) & (position < micro)
        keep = mask_for(index)
        given = lax.dynamic_slice_in_dim(whole, index * rows, rows).astype(jnp.float32)
        inputs = jnp.where(
            first,
            given,
            lax.dynamic_index_in_dim(stored_rows, index, 0, keepdims=False).astype(jnp.float32),
        )
        grad_out = jnp.where(first, received_grad.astype(jnp.float32), given)
        pairs_now = lax.dynamic_index_in_dim(stored_pairs, index, 0, keepdims=False)

        def stored_source():
            return pairs_now

        grad_inputs, section_terms, cross_terms, grad_pairs = layer_backward(
            inputs, keep, weights, cross_weights, stored_source, later, image_rows, grad_out
        )
        own_image = lax.dynamic_slice_in_dim(image, index * captions, captions)
        own_pair_grad = jnp.where(first, received_pair_grad, grad_pairs[:, half_image:])
        flat_pair_grad = own_pair_grad.reshape(captions * half_image, 2 * width)
        image_piece = input_grad(flat_pair_grad, cross_keys_full).reshape(
            captions, half_image, width
        )
        keys_term = weight_grad(own_image.reshape(captions * half_image, width), flat_pair_grad)
        section_sums = tuple(
            (
                jnp.where(valid, total + term, total)
                for total, term in zip(section_sums, section_terms)
            )
        )
        cross_now = (cross_terms[0], cross_terms[1], cross_terms[2], keys_term, cross_terms[3])
        cross_sums = tuple(
            (jnp.where(valid, total + term, total) for total, term in zip(cross_sums, cross_now))
        )
        image_grads = jnp.where(
            valid,
            lax.dynamic_update_slice_in_dim(image_grads, image_piece, index * captions, 0),
            image_grads,
        )
        text_grads = jnp.where(
            valid & first,
            lax.dynamic_update_slice_in_dim(text_grads, grad_inputs, index * rows, 0),
            text_grads,
        )
        if moment < micro:
            received_grad, received_pair_grad = from_behind(
                (grad_inputs.astype(jnp.bfloat16), grad_pairs[:, :half_image]), "section", -1
            )
    final = jnp.where(first, text_grads, outputs)
    halves = lax.all_to_all(final[None], "section", split_axis=2, concat_axis=0, tiled=True)
    section_grads = (
        lax.psum_scatter(section_sums[0][None], "dp", scatter_dimension=1, tiled=True),
        lax.psum_scatter(section_sums[1][None], "dp", scatter_dimension=1, tiled=True),
        lax.psum_scatter(section_sums[2][None], "dp", scatter_dimension=1, tiled=True),
        lax.psum_scatter(section_sums[3][None], "dp", scatter_dimension=1, tiled=True),
        lax.psum_scatter(section_sums[4][None], "dp", scatter_dimension=1, tiled=True),
        lax.psum_scatter(section_sums[5][None], "dp", scatter_dimension=1, tiled=True),
        lax.psum_scatter(section_sums[6][None], "dp", scatter_dimension=1, tiled=True),
        lax.psum_scatter(section_sums[7][None], "dp", scatter_dimension=1, tiled=True),
        lax.psum_scatter(section_sums[8][None], "dp", scatter_dimension=1, tiled=True),
        lax.psum_scatter(section_sums[9][None], "dp", scatter_dimension=1, tiled=True),
    )
    cross_grads = (
        lax.psum_scatter(cross_sums[0], ("section", "dp"), scatter_dimension=0, tiled=True),
        lax.psum_scatter(cross_sums[1], ("section", "dp"), scatter_dimension=0, tiled=True),
        lax.psum_scatter(cross_sums[2], ("section", "dp"), scatter_dimension=0, tiled=True),
        lax.psum_scatter(cross_sums[3], ("section", "dp"), scatter_dimension=0, tiled=True),
        lax.psum_scatter(cross_sums[4], ("section", "dp"), scatter_dimension=0, tiled=True),
    )
    return (
        halves[1],
        halves[0],
        image_grads,
        section_grads[0],
        section_grads[1],
        section_grads[2],
        section_grads[3],
        section_grads[4],
        section_grads[5],
        section_grads[6],
        section_grads[7],
        section_grads[8],
        section_grads[9],
        cross_grads[0],
        cross_grads[1],
        cross_grads[2],
        cross_grads[3],
        cross_grads[4],
    )


def solution(mesh):
    placed = (
        P("dp", "section"),
        P("dp", "section", None),
        P("dp"),
        P("section", "dp"),
        P("section", "dp"),
        P("section", "dp", None),
        P("section", "dp", None),
        P("section", "dp"),
        P("section", "dp"),
        P("section", "dp", None),
        P("section", "dp"),
        P("section", "dp", None),
        P("section", "dp"),
        P(("section", "dp")),
        P(("section", "dp")),
        P(("section", "dp"), None),
        P(("section", "dp"), None),
        P(("section", "dp"), None),
        P("dp", "section"),
    )
    return jax.shard_map(
        body,
        mesh=mesh,
        in_specs=placed,
        out_specs=(
            P("dp", "section"),
            P("dp", "section"),
            P("dp", "section", None),
            P("section", "dp"),
            P("section", "dp"),
            P("section", "dp", None),
            P("section", "dp", None),
            P("section", "dp"),
            P("section", "dp"),
            P("section", "dp", None),
            P("section", "dp"),
            P("section", "dp", None),
            P("section", "dp"),
            P(("section", "dp")),
            P(("section", "dp")),
            P(("section", "dp"), None),
            P(("section", "dp"), None),
            P(("section", "dp"), None),
        ),
        check_vma=False,
    )
```

profile of v0, /device:TPU:0, one launch (start us, length us, event | category | flops | bytes accessed | tf_op | source)
XLA Modules:
  0.0 2187.8 jit_solution(8722213138479659365)
XLA Ops:
  13.8 4.2 all-to-all-start
  21.4 62.8 %all-reduce.13 = (bf16[3072]{0:T(1024)(128)(2,1)S(1)}, bf16[768]{0:T(1024)(128)(2,1)S(1)}, bf16[768]{0:T(1024)(128)(2,1)S(1)}, bf16[768]{0:T(1024)(128)(2,1)S(1)...) all-reduce(bf16[3072]{0:T(1024)(128)(2,1)S(1)} %dynamic-update-slic, ...), channel_id=1, replica_groups=mesh['section'=2,'dp'=16] {'dp'}, use_global_device_ids=true, to_apply=%add.7 | all-reduce | flops 6912 | bytes 27648
  85.9 37.0 %all-reduce.12 = (bf16[768]{0:T(1024)(128)(2,1)}, bf16[768]{0:T(1024)(128)(2,1)}) all-reduce(bf16[768]{0:T(1024)(128)(2,1)S(1)} %dynamic-update-slice.10, bf16[768]{0:T(1024)(128)(2,1)S(1)} %dynamic-update-slice.11), channel_id=1, replica_groups=mesh['section'=2,'dp'=16] {'section','dp'}, use_global_device_ids=true, to_apply=%add.3 | all-reduce | flops 1536 | bytes 6144
  136.1 20.1 all-gather.14.cloned.1.call-done
  156.2 55.8 %all-gather.16.cloned.1.call-done = bf16[768,768]{1,0:T(8,128)(2,1)} async-done(((bf16[24,768]{1,0:T(8,128)(2,1)}), bf16[768,768]{1,0:T(8,128)(2,1)}) %all-gather.16.cloned.1.call-update) | async-done | bytes 1179664 | tf_op jit(solution)/shard_map/all_gather | solution.py:346
  212.0 58.9 %all-gather.12.cloned.1.call-done = bf16[768,1536]{1,0:T(8,128)(2,1)} async-done(((bf16[24,1536]{1,0:T(8,128)(2,1)}), bf16[768,1536]{1,0:T(8,128)(2,1)}) %all-gather.12.cloned.1.call-update) | async-done | bytes 2359312 | tf_op jit(solution)/shard_map/all_gather | solution.py:345
  272.8 52.7 %all-gather.20.cloned.1.call-done = bf16[1,3072,768]{2,1,0:T(8,128)(2,1)} async-done(((bf16[1,192,768]{2,1,0:T(8,128)(2,1)}), bf16[1,3072,768]{2,1,0:T(8,128)(2,1)}) %all-gather.20.cloned.1.call-update) | async-done | bytes 4718608 | tf_op jit(solution)/shard_map/all_gather | solution.py:337
  325.4 54.3 %all-gather.18.cloned.1.call-done = bf16[1,768,3072]{2,1,0:T(8,128)(2,1)} async-done(((bf16[1,48,3072]{2,1,0:T(8,128)(2,1)}), bf16[1,768,3072]{2,1,0:T(8,128)(2,1)}) %all-gather.18.cloned.1.call-update) | async-done | bytes 4718608 | tf_op jit(solution)/shard_map/all_gather | solution.py:335
  379.7 9.4 fusion.317
  389.0 4.0 collective-permute-start
  436.3 9.5 select_dynamic-update-slice_fusion.3
  445.8 58.4 %collective-permute-start.2 = (bf16[128,768]{1,0:T(8,128)(2,1)}, bf16[128,768]{1,0:T(8,128)(2,1)S(1)}, u32[]{:S(2)}, u32[]{:S(2)}) collective-permute-start(bf16[128,768]{1,0:T(8,128)(2,1)} %get-tuple-element.756), channel_id=1, source_target_pairs={{0,16},{1,17},{2,18},{3,19},{4,20},{5,21},{6,22},{7,23},{8,24},{9,... | collective-permute-start | bytes 589832 | tf_op jit(solution)/shard_map/ppermute | solution.py:18
  504.3 4.4 constant_dynamic-update-slice_fusion.1
  568.5 4.5 constant_dynamic-update-slice_fusion
  574.1 10.6 conditional.12
  588.2 3.4 fusion.156
  591.7 8.0 convert_reduce_fusion.2
  599.7 3.7 multiply_reduce_fusion.29
  605.5 15.1 conditional.13
  635.2 3.8 copy.377
  652.4 120.9 %collective-permute-done.4 = bf16[128,768]{1,0:T(8,128)(2,1)S(1)} collective-permute-done((bf16[128,768]{1,0:T(8,128)(2,1)S(1)}, bf16[128,768]{1,0:T(8,128)(2,1)S(1)}, u32[]{:S(2)}, u32[]{:S(2)}) %collective-permute-start.4) | collective-permute-done | bytes 196640 | tf_op jit(solution)/shard_map/ppermute | solution.py:18
  780.8 3.4 reshape.1001
  804.5 10.6 conditional.14
  818.6 3.4 fusion.159
  822.1 8.1 convert_reduce_fusion.1
  830.2 3.7 multiply_reduce_fusion.28
  836.0 8.5 conditional.15
  859.0 3.8 copy.398
  876.8 68.4 %collective-permute-done.5 = bf16[128,768]{1,0:T(8,128)(2,1)} collective-permute-done((bf16[128,768]{1,0:T(8,128)(2,1)}, bf16[128,768]{1,0:T(8,128)(2,1)}, u32[]{:S(2)}, u32[]{:S(2)}) %collective-permute-start.5) | collective-permute-done | bytes 196640 | tf_op jit(solution)/shard_map/ppermute | solution.py:18
  952.9 3.4 reshape.1003
  976.5 10.6 conditional.16
  990.7 3.4 fusion.162
  994.2 8.2 convert_reduce_fusion
  1002.4 3.7 multiply_reduce_fusion.27
  1009.1 7.8 conditional.17
  1031.5 3.8 copy.419
  1038.5 3.9 multiply_reduce_fusion.30
  1053.6 3.5 add_select_fusion.10
  1057.1 4.2 add_select_fusion.8
  1068.3 4.4 copy.422
  1076.4 4.4 copy.424
  1087.4 106.1 %collective-permute-done.6 = bf16[2,288,1536]{2,1,0:T(8,128)(2,1)} collective-permute-done((bf16[2,288,1536]{2,1,0:T(8,128)(2,1)}, bf16[2,288,1536]{2,1,0:T(8,128)(2,1)}, u32[]{:S(2)}, u32[]{:S(2)}) %collective-permute-start.6) | collective-permute-done | bytes 1769504 | tf_op jit(solution)/shard_map/ppermute | solution.py:18
  1193.5 3.5 fusion.327
  1197.0 31.1 %collective-permute-done.7 = bf16[2,288,1536]{2,1,0:T(8,128)(2,1)S(1)} collective-permute-done((bf16[2,288,1536]{2,1,0:T(8,128)(2,1)S(1)}, bf16[2,288,1536]{2,1,0:T(8,128)(2,1)S(1)}, u32[]{:S(2)}, u32[]{:S(2)}) %collective-permute-start.7) | collective-permute-done | bytes 1769504 | tf_op jit(solution)/shard_map/ppermute | solution.py:18
  1229.3 4.9 add_select_fusion.6
  1238.1 4.7 fusion.119
  1249.1 5.7 fusion.117
  1256.2 4.6 fusion.347
  1260.8 4.6 fusion.348
  1265.4 8.0 fusion.118
  1283.0 8.8 fusion.323
  1297.0 4.6 all-to-all-start.1
  1303.0 40.0 %all-reduce.11 = (f32[768]{0:T(1024)S(1)}, f32[768]{0:T(1024)S(1)}) all-reduce(f32[768]{0:T(1024)S(1)} %add_select_fusion.16, f32[768]{0:T(1024)S(1)} %add_select_fusion.14), channel_id=12, replica_groups=mesh['section'=2,'dp'=16] {'section','dp'}, use_global_device_ids=true, to_apply=%region_142.143.clone | all-reduce | flops 1536 | bytes 12288
  1349.5 55.6 %reduce-scatter.50.cloned.1.call-done = f32[48,1]{1,0:T(8,128)} async-done(((f32[768,1]{1,0:T(8,128)}), f32[48,1]{1,0:T(8,128)}) %reduce-scatter.50.cloned.1.call-update) | async-done | bytes 208
  1406.4 61.3 %reduce-scatter.48.cloned.1.call-done = f32[192,1]{1,0:T(8,128)} async-done(((f32[3072,1]{1,0:T(8,128)}), f32[192,1]{1,0:T(8,128)}) %reduce-scatter.48.cloned.1.call-update) | async-done | bytes 784
  1474.3 5.7 select_dynamic-update-slice_fusion.1
  1480.0 4.3 select_dynamic-update-slice_fusion
  1484.4 87.1 %reduce-scatter.34.cloned.1.call-done = f32[24,768]{1,0:T(8,128)} async-done(((f32[768,768]{1,0:T(8,128)}), f32[24,768]{1,0:T(8,128)}) %reduce-scatter.34.cloned.1.call-update) | async-done | bytes 73744 | tf_op jit(solution)/shard_map/reduce_scatter | solution.py:488
  1571.5 104.6 %reduce-scatter.38.cloned.1.call-done = f32[24,768]{1,0:T(8,128)} async-done(((f32[768,768]{1,0:T(8,128)}), f32[24,768]{1,0:T(8,128)}) %reduce-scatter.38.cloned.1.call-update) | async-done | bytes 73744 | tf_op jit(solution)/shard_map/reduce_scatter | solution.py:490
  1676.1 66.3 %reduce-scatter.28.cloned.1.call-done = f32[1,48,768]{2,1,0:T(8,128)} async-done(((f32[1,768,768]{2,1,0:T(8,128)}), f32[1,48,768]{2,1,0:T(8,128)}) %reduce-scatter.28.cloned.1.call-update) | async-done | bytes 147472 | tf_op jit(solution)/shard_map/reduce_scatter | solution.py:477
  1742.4 112.9 %reduce-scatter.36.cloned.1.call-done = f32[24,1536]{1,0:T(8,128)} async-done(((f32[768,1536]{1,0:T(8,128)}), f32[24,1536]{1,0:T(8,128)}) %reduce-scatter.36.cloned.1.call-update) | async-done | bytes 147472 | tf_op jit(solution)/shard_map/reduce_scatter | solution.py:489
  1855.3 93.6 %reduce-scatter.26.cloned.1.call-done = f32[1,48,2304]{2,1,0:T(8,128)} async-done(((f32[1,768,2304]{2,1,0:T(8,128)}), f32[1,48,2304]{2,1,0:T(8,128)}) %reduce-scatter.26.cloned.1.call-update) | async-done | bytes 442384 | tf_op jit(solution)/shard_map/reduce_scatter | solution.py:476
  1948.9 116.2 %reduce-scatter.30.cloned.1.call-done = f32[1,48,3072]{2,1,0:T(8,128)} async-done(((f32[1,768,3072]{2,1,0:T(8,128)}), f32[1,48,3072]{2,1,0:T(8,128)}) %reduce-scatter.30.cloned.1.call-update) | async-done | bytes 589840 | tf_op jit(solution)/shard_map/reduce_scatter | solution.py:480
  2065.1 115.7 %reduce-scatter.32.cloned.1.call-done = f32[1,192,768]{2,1,0:T(8,128)} async-done(((f32[1,3072,768]{2,1,0:T(8,128)}), f32[1,192,768]{2,1,0:T(8,128)}) %reduce-scatter.32.cloned.1.call-update) | async-done | bytes 589840 | tf_op jit(solution)/shard_map/reduce_scatter | solution.py:482
  (680 shorter events, 401.7 us)
Async XLA Ops:
  7.2 10.8 copy-start.202
  7.2 12.7 copy-start.173
  7.2 12.8 copy-start.195
  7.2 13.0 copy-start.196
  7.2 13.2 copy-start.197
  7.2 13.4 copy-start.198
  7.3 13.7 copy-start.199
  7.3 78.1 %copy-start.200 = (bf16[24]{0:T(256)(128)(2,1)S(1)}, bf16[24]{0:T(256)(128)(2,1)}, u32[]{:S(2)}) copy-start(bf16[24]{0:T(256)(128)(2,1)} %param.50) | copy-start | bytes 148
  7.3 78.4 %copy-start.201 = (bf16[24]{0:T(256)(128)(2,1)S(1)}, bf16[24]{0:T(256)(128)(2,1)}, u32[]{:S(2)}) copy-start(bf16[24]{0:T(256)(128)(2,1)} %param.51) | copy-start | bytes 148
  7.3 115.6 %copy-start.125 = (s32[4]{0:T(128)S(1)}, s32[4]{0:T(128)}, u32[]{:S(2)}) copy-start(s32[4]{0:T(128)} %param.39) | copy-start | bytes 52
  7.3 115.6 %copy-start.42 = (bf16[4,288,768]{2,1,0:T(8,128)(2,1)S(1)}, bf16[4,288,768]{2,1,0:T(8,128)(2,1)}, u32[]{:S(2)}) copy-start(bf16[4,288,768]{2,1,0:T(8,128)(2,1)} %param.38) | copy-start | bytes 5308420
  7.3 118.6 %all-gather.8.cloned.1.call-start = ((), (), s32[]{:S(2)}) async-start(), calls=%async_computation.15 | async-start | bytes 3760128 | tf_op jit(solution)/shard_map/all_gather | solution.py:331
  8.0 126.4 %all-gather.10.cloned.1.call-start = ((), (), s32[]{:S(2)}) async-start(), calls=%async_computation.16 | async-start | bytes 1253376 | tf_op jit(solution)/shard_map/all_gather | solution.py:332
  8.8 147.4 %all-gather.14.cloned.1.call-start = ((), (), s32[]{:S(2)}) async-start(), calls=%async_computation.18 | async-start | bytes 1216512 | tf_op jit(solution)/shard_map/all_gather | solution.py:344
  9.5 202.5 %all-gather.16.cloned.1.call-start = ((), (), s32[]{:S(2)}) async-start(), calls=%async_computation.19 | async-start | bytes 1216512 | tf_op jit(solution)/shard_map/all_gather | solution.py:346
  10.1 260.9 %all-gather.12.cloned.1.call-start = ((), (), s32[]{:S(2)}) async-start(), calls=%async_computation.17 | async-start | bytes 2433024 | tf_op jit(solution)/shard_map/all_gather | solution.py:345
  10.7 314.7 %all-gather.20.cloned.1.call-start = ((), (), s32[]{:S(2)}) async-start(), calls=%async_computation.21 | async-start | bytes 5013504 | tf_op jit(solution)/shard_map/all_gather | solution.py:337
  11.3 368.4 %all-gather.18.cloned.1.call-start = ((), (), s32[]{:S(2)}) async-start(), calls=%async_computation.20 | async-start | bytes 5013504 | tf_op jit(solution)/shard_map/all_gather | solution.py:335
  13.8 111.2 %all-to-all-start = ((bf16[2,256,384]{2,1,0:T(8,128)(2,1)}), bf16[2,256,384]{2,1,0:T(8,128)(2,1)S(1)}, u32[]{:S(2)}, u32[]{:S(2)}) async-start(bf16[2,256,384]{2,1,0:T(8,128)(2,1)} %pad_maximum_fusion.5), calls=%async_computation | async-start | bytes 786432 | tf_op jit(solution)/shard_map/all_to_all | solution.py:325
  18.0 1326.1 %reduce-scatter.40.cloned.1.call-start = ((), (), s32[]{:S(2)}) async-start(), calls=%async_computation.29 | async-start | bytes 417792
  124.0 147.0 %copy-start.56 = (bf16[2,288,768]{2,1,0:T(8,128)(2,1)}, bf16[2,288,768]{2,1,0:T(8,128)(2,1)S(1)}, u32[]{:S(2)}) copy-start(bf16[2,288,768]{2,1,0:T(8,128)(2,1)S(1)} %get-tuple-element.730) | copy-start | bytes 2654212
  125.5 9.0 copy-start.1
  272.8 128.3 %copy-start = (bf16[1,768,2304]{2,1,0:T(8,128)(2,1)S(1)}, bf16[1,768,2304]{2,1,0:T(8,128)(2,1)}, u32[]{:S(2)}) copy-start(bf16[1,768,2304]{2,1,0:T(8,128)(2,1)} %all-gather.8.cloned.1.call-done) | copy-start | bytes 10616836
  389.0 8.9 collective-permute-start
  393.1 35.5 %collective-permute-start.1 = (bf16[2,288,768]{2,1,0:T(8,128)(2,1)}, bf16[2,288,768]{2,1,0:T(8,128)(2,1)}, u32[]{:S(2)}, u32[]{:S(2)}) collective-permute-start(bf16[2,288,768]{2,1,0:T(8,128)(2,1)} %copy-done.56), channel_id=1, source_target_pairs={{0,16},{1,17},{2,18},{3,19},{4,20},{5,21},{6,22},{7,23},{8,24},{9,... | collective-permute-start | bytes 2654216 | tf_op jit(solution)/shard_map/ppermute | solution.py:18
  395.3 170.7 %collective-permute-start.3 = (bf16[2,288,768]{2,1,0:T(8,128)(2,1)}, bf16[2,288,768]{2,1,0:T(8,128)(2,1)}, u32[]{:S(2)}, u32[]{:S(2)}) collective-permute-start(bf16[2,288,768]{2,1,0:T(8,128)(2,1)} %get-tuple-element.729), channel_id=1, source_target_pairs={{0,16},{1,17},{2,18},{3,19},{4,20},{5,21},{6,22},{7,23},{8,24},{9,... | collective-permute-start | bytes 2654216 | tf_op jit(solution)/shard_map/ppermute | solution.py:18
  445.8 63.5 %collective-permute-start.2 = (bf16[128,768]{1,0:T(8,128)(2,1)}, bf16[128,768]{1,0:T(8,128)(2,1)S(1)}, u32[]{:S(2)}, u32[]{:S(2)}) collective-permute-start(bf16[128,768]{1,0:T(8,128)(2,1)} %get-tuple-element.756), channel_id=1, source_target_pairs={{0,16},{1,17},{2,18},{3,19},{4,20},{5,21},{6,22},{7,23},{8,24},{9,... | collective-permute-start | bytes 589832 | tf_op jit(solution)/shard_map/ppermute | solution.py:18
  587.0 16.4 copy-start.116
  588.2 15.2 copy-start.143
  588.2 11.5 slice-start
  645.0 128.2 %copy-start.38 = (bf16[128,768]{1,0:T(8,128)(2,1)S(1)}, bf16[128,768]{1,0:T(8,128)(2,1)}, u32[]{:S(2)}) copy-start(bf16[128,768]{1,0:T(8,128)(2,1)} %copy-done.37) | copy-start | bytes 589828
  648.1 125.1 %collective-permute-start.4 = (bf16[128,768]{1,0:T(8,128)(2,1)S(1)}, bf16[128,768]{1,0:T(8,128)(2,1)S(1)}, u32[]{:S(2)}, u32[]{:S(2)}) collective-permute-start(bf16[128,768]{1,0:T(8,128)(2,1)S(1)} %get-tuple-element.751), channel_id=1, source_target_pairs={{16,0},{17,1},{18,2},{19,3},{20,4},{21,5},{22,6},{23,7},{24,8},{25... | collective-permute-start | bytes 589832 | tf_op jit(solution)/shard_map/ppermute | solution.py:18
  817.4 16.5 copy-start.121
  818.6 15.3 copy-start.148
  818.6 11.6 slice-start.2
  822.1 8.1 copy-start.82
  871.7 73.5 %collective-permute-start.5 = (bf16[128,768]{1,0:T(8,128)(2,1)}, bf16[128,768]{1,0:T(8,128)(2,1)}, u32[]{:S(2)}, u32[]{:S(2)}) collective-permute-start(bf16[128,768]{1,0:T(8,128)(2,1)} %get-tuple-element.749), channel_id=1, source_target_pairs={{16,0},{17,1},{18,2},{19,3},{20,4},{21,5},{22,6},{23,7},{24,8},{25... | collective-permute-start | bytes 589832 | tf_op jit(solution)/shard_map/ppermute | solution.py:18
  876.8 70.8 %copy-start.123 = (f32[128]{0:T(128)}, f32[128]{0:T(128)S(1)}, u32[]{:S(2)}) copy-start(f32[128]{0:T(128)S(1)} %broadcast_multiply_fusion.11) | copy-start | bytes 1540
  989.5 16.6 copy-start.152
  990.7 15.4 copy-start.160
  990.7 11.7 slice-start.4
  994.1 8.2 copy-start.84
  994.2 8.2 slice-start.5
  1043.5 302.0 %reduce-scatter.42.cloned.1.call-start = ((), (), s32[]{:S(2)}) async-start(), calls=%async_computation.30 | async-start | bytes 417792
  1045.3 301.5 %reduce-scatter.44.cloned.1.call-start = ((), (), s32[]{:S(2)}) async-start(), calls=%async_computation.31 | async-start | bytes 417792
  1046.4 301.8 %reduce-scatter.46.cloned.1.call-start = ((), (), s32[]{:S(2)}) async-start(), calls=%async_computation.32 | async-start | bytes 417792
  1047.4 357.6 %reduce-scatter.50.cloned.1.call-start = ((), (), s32[]{:S(2)}) async-start(), calls=%async_computation.34 | async-start | bytes 417792
  1048.5 419.2 %reduce-scatter.48.cloned.1.call-start = ((), (), s32[]{:S(2)}) async-start(), calls=%async_computation.33 | async-start | bytes 1671168
  1053.5 518.0 %reduce-scatter.34.cloned.1.call-start = ((), (), s32[]{:S(2)}) async-start(), calls=%async_computation.26 | async-start | bytes 2433024 | tf_op jit(solution)/shard_map/reduce_scatter | solution.py:488
  1057.1 619.0 %reduce-scatter.38.cloned.1.call-start = ((), (), s32[]{:S(2)}) async-start(), calls=%async_computation.28 | async-start | bytes 2433024 | tf_op jit(solution)/shard_map/reduce_scatter | solution.py:490
  1061.4 681.0 %reduce-scatter.28.cloned.1.call-start = ((), (), s32[]{:S(2)}) async-start(), calls=%async_computation.23 | async-start | bytes 2506752 | tf_op jit(solution)/shard_map/reduce_scatter | solution.py:477
  1068.3 787.1 %reduce-scatter.36.cloned.1.call-start = ((), (), s32[]{:S(2)}) async-start(), calls=%async_computation.27 | async-start | bytes 4866048 | tf_op jit(solution)/shard_map/reduce_scatter | solution.py:489
  1075.1 118.3 %collective-permute-start.6 = (bf16[2,288,1536]{2,1,0:T(8,128)(2,1)}, bf16[2,288,1536]{2,1,0:T(8,128)(2,1)}, u32[]{:S(2)}, u32[]{:S(2)}) collective-permute-start(bf16[2,288,1536]{2,1,0:T(8,128)(2,1)} %slice.207), channel_id=1, source_target_pairs={{16,0},{17,1},{18,2},{19,3},{20,4},{21,5},{22,6},{23,7},{24,8},{25... | collective-permute-start | bytes 5308424 | tf_op jit(solution)/shard_map/ppermute | solution.py:18
  1080.9 112.6 %copy-start.26 = (bf16[2,576,1536]{2,1,0:T(8,128)(2,1)}, bf16[2,576,1536]{2,1,0:T(8,128)(2,1)S(1)}, u32[]{:S(2)}) copy-start(bf16[2,576,1536]{2,1,0:T(8,128)(2,1)S(1)} %copy.424) | copy-start | bytes 10616836
  1081.0 112.5 %copy-start.44 = (bf16[4,288,768]{2,1,0:T(8,128)(2,1)S(1)}, bf16[4,288,768]{2,1,0:T(8,128)(2,1)}, u32[]{:S(2)}) copy-start(bf16[4,288,768]{2,1,0:T(8,128)(2,1)} %param.38) | copy-start | bytes 5308420
  1081.0 147.1 %collective-permute-start.7 = (bf16[2,288,1536]{2,1,0:T(8,128)(2,1)S(1)}, bf16[2,288,1536]{2,1,0:T(8,128)(2,1)S(1)}, u32[]{:S(2)}, u32[]{:S(2)}) collective-permute-start(bf16[2,288,1536]{2,1,0:T(8,128)(2,1)S(1)} %slice.209), channel_id=1, source_target_pairs={{16,0},{17,1},{18,2},{19,3},{20,4},{21,5},{22,6},{23,7},{24,8},{25... | collective-permute-start | bytes 5308424 | tf_op jit(solution)/shard_map/ppermute | solution.py:18
  1234.3 714.6 %reduce-scatter.26.cloned.1.call-start = ((), (), s32[]{:S(2)}) async-start(), calls=%async_computation.22 | async-start | bytes 7520256 | tf_op jit(solution)/shard_map/reduce_scatter | solution.py:476
  1242.8 822.2 %reduce-scatter.30.cloned.1.call-start = ((), (), s32[]{:S(2)}) async-start(), calls=%async_computation.24 | async-start | bytes 10027008 | tf_op jit(solution)/shard_map/reduce_scatter | solution.py:480
  1254.8 925.9 %reduce-scatter.32.cloned.1.call-start = ((), (), s32[]{:S(2)}) async-start(), calls=%async_computation.25 | async-start | bytes 10027008 | tf_op jit(solution)/shard_map/reduce_scatter | solution.py:482
  1283.0 8.8 copy-start.175
  1283.0 8.8 copy-start.178
  1283.0 8.8 copy-start.86
  1297.0 177.3 %copy-start.27 = (bf16[2,576,1536]{2,1,0:T(8,128)(2,1)S(1)}, bf16[2,576,1536]{2,1,0:T(8,128)(2,1)}, u32[]{:S(2)}) copy-start(bf16[2,576,1536]{2,1,0:T(8,128)(2,1)} %copy-done.26) | copy-start | bytes 10616836
  1297.0 172.2 %all-to-all-start.1 = ((f32[1,256,768]{1,0,2:T(1,128)}), f32[1,256,768]{1,0,2:T(1,128)}, u32[]{:S(2)}, u32[]{:S(2)}) async-start(f32[1,256,768]{1,0,2:T(1,128)} %copy.420), calls=%async_computation.1 | async-start | bytes 1572864 | tf_op jit(solution)/shard_map/all_to_all | solution.py:472
  (128 other events, 344.1 us)
Sparse Core Ops, SparseCore 0:
  10.4 50.5 all-gather.7
  63.3 36.8 all-gather.9
  103.1 53.0 all-gather.13
  159.0 53.0 all-gather.15
  214.8 56.1 all-gather.11
  273.1 52.2 all-gather.19
  327.7 51.9 all-gather.17
  1043.6 128.3 reduce-scatter.39
  1175.9 54.6 reduce-scatter.41
  1233.9 54.5 reduce-scatter.43
  1292.4 54.5 reduce-scatter.45
  1350.4 54.6 reduce-scatter.49
  1409.2 58.4 reduce-scatter.47
  1473.4 98.0 reduce-scatter.33
  1578.1 98.0 reduce-scatter.37
  1680.3 62.0 reduce-scatter.27
  1749.2 106.0 reduce-scatter.35
  1859.7 89.1 reduce-scatter.25
  1954.2 110.8 reduce-scatter.29
  2069.6 111.0 reduce-scatter.31
where the time goes:
time: 2200 us; the launch traced here: 2190 us
  waiting for transfers between devices  1390 us (63%)
  local copies, waits for them, and re-layouts  255 us (12%)
  matrix products  219 us (10%)
  blocking collectives  140 us (6%)
  starting transfers between devices  82.6 us (4%)
  other arithmetic  73 us (3%)
    ppermute x8, waiting for transfers between devices, from_behind(): lax.ppermute(value, axis, [(source, source + steps) for source in range(l...  327 us
    unnamed x3, blocking collectives  140 us
    unnamed x26, waiting for transfers between devices  121 us
    reduce_scatter x1, waiting for transfers between devices, body(): lax.psum_scatter(section_sums[6][None], 'dp', scatter_dimension=1, tiled=...  116 us
    reduce_scatter x1, waiting for transfers between devices, body(): lax.psum_scatter(section_sums[8][None], 'dp', scatter_dimension=1, tiled=...  116 us
    reduce_scatter x1, waiting for transfers between devices, body(): lax.psum_scatter(cross_sums[3], ('section', 'dp'), scatter_dimension=0, t...  113 us
    reduce_scatter x1, waiting for transfers between devices, body(): lax.psum_scatter(cross_sums[4], ('section', 'dp'), scatter_dimension=0, t...  105 us
    reduce_scatter x1, waiting for transfers between devices, body(): lax.psum_scatter(section_sums[2][None], 'dp', scatter_dimension=1, tiled=...  93.6 us
  transfers between devices with their start and end apart: 30, of which 19 were waited for; matrix products, arithmetic and copies ran while one was open for 12% of the time, Pallas kernels for 0%

commit v1 on v0

v1 whole, which is shorter than its diff:
```python
import jax
import jax.numpy as jnp
from jax import lax
from jax.sharding import PartitionSpec as P

HEADS = 12
HEAD_DIM = 64
EPS = 1e-05
MASKED = -1000000000.0
F32 = jnp.float32
BF16 = jnp.bfloat16


def swap(value):
    return lax.ppermute(value, "section", [(0, 1), (1, 0)])


def side(own, other, section, axis):
    first = jnp.where(section == 0, own, other)
    later = jnp.where(section == 0, other, own)
    return jnp.concatenate([first, later], axis)


def pick(section, first, later):
    return jnp.where(section == 0, first, later)


def low(values):
    return values.astype(BF16)


def norm_stats(values):
    mean = jnp.mean(values, -1, keepdims=True)
    centred = values - mean
    scale = lax.rsqrt(jnp.mean(centred * centred, -1, keepdims=True) + EPS)
    return centred * scale, scale


def norm(values, gain, shift):
    unit, _ = norm_stats(values)
    return low(unit * gain + shift)


def norm_back(values, gain, grad):
    unit, scale = norm_stats(values)
    wide = grad * gain
    inner = wide - jnp.mean(wide, -1, keepdims=True) - unit * jnp.mean(wide * unit, -1, keepdims=True)
    return inner * scale, jnp.sum(grad * unit, 0), jnp.sum(grad, 0)


def dot(left, right):
    return jnp.dot(left, right, preferred_element_type=F32)


def dot_tn(left, right):
    return lax.dot_general(left, right, (((0,), (0,)), ((), ())), preferred_element_type=F32)


def dot_nt(left, right):
    return lax.dot_general(left, right, (((1,), (1,)), ((), ())), preferred_element_type=F32)


def gelu(values):
    return 0.5 * values * (1.0 + lax.erf(values * 0.5**0.5))


def gelu_slope(values):
    return 0.5 * (1.0 + lax.erf(values * 0.5**0.5)) + values * jnp.exp(-0.5 * values * values) * 0.3989422804014327


def softmax_rows(scores):
    raised = jnp.exp(scores - jnp.max(scores, -1, keepdims=True))
    return raised / jnp.sum(raised, -1, keepdims=True)


def split_heads(values, captions):
    rows, width = values.shape
    return values.reshape(captions, rows // captions, width // HEAD_DIM, HEAD_DIM)


def scores_of(queries, keys):
    return jnp.einsum("cqhd,ckhd->chqk", queries, keys, preferred_element_type=F32) * HEAD_DIM**-0.5


def mix(chances, values):
    return jnp.einsum("chqk,ckhd->cqhd", chances, values, preferred_element_type=F32)


def attend_back(queries, keys, values, chances, slope):
    grad_low = low(slope)
    scale = HEAD_DIM**-0.5
    query_part = jnp.einsum("chqk,ckhd->cqhd", grad_low, keys, preferred_element_type=F32) * scale
    key_part = jnp.einsum("chqk,cqhd->ckhd", grad_low, queries, preferred_element_type=F32) * scale
    return query_part, key_part


def body(
    text,
    image,
    lengths,
    self_gain,
    self_shift,
    heads_in,
    heads_out,
    feed_gain,
    feed_shift,
    up_weight,
    up_bias,
    down_weight,
    down_bias,
    cross_gain,
    cross_shift,
    cross_query,
    cross_keys,
    cross_out,
    cotangent,
):
    section = lax.axis_index("section")
    count = lax.axis_size("dp")
    captions, half_image, width = image.shape
    rows = text.shape[0]
    slots = rows // captions
    piece = heads_in.shape[1]
    cross_piece = cross_query.shape[0]
    half = width // 2
    folds = down_weight.shape[1] // (2 * piece)
    half_ff = folds * width

    def halves(index):
        into = heads_in[0].reshape(piece, 3, 2, half)[:, :, index].reshape(piece, 3 * half)
        up = up_weight[0].reshape(piece, count, 2, folds, piece)[:, :, index]
        up = up.transpose(0, 2, 1, 3).reshape(piece, half_ff)
        down = down_weight[0].reshape(2, folds, piece, width)[index]
        down = down.transpose(1, 0, 2).reshape(piece, folds * width)
        bias = up_bias[0].reshape(2, folds, piece)[index]
        vectors = jnp.stack([self_gain[0], self_shift[0], feed_gain[0], feed_shift[0], down_bias[0]] + [bias[i] for i in range(folds)], 1)
        return jnp.concatenate([into, heads_out[0], vectors], 1), jnp.concatenate([up, down], 1)

    attn_0, feed_0 = halves(0)
    attn_1, feed_1 = halves(1)
    own_attn, own_feed = pick(section, attn_0, attn_1), pick(section, feed_0, feed_1)
    got_attn, got_feed = swap(pick(section, attn_1, attn_0)), swap(pick(section, feed_1, feed_0))
    layer_attn = (pick(section, own_attn, got_attn), pick(section, got_attn, own_attn))
    layer_feed = (pick(section, own_feed, got_feed), pick(section, got_feed, own_feed))
    own_cross = jnp.concatenate([cross_query, cross_keys, cross_out, cross_gain[:, None], cross_shift[:, None]], 1)
    both_cross = side(own_cross, swap(own_cross), section, 1)
    cross_width = own_cross.shape[1]

    def gather(value):
        return lax.all_gather(value, "dp", axis=0, tiled=True)

    attn = [gather(layer_attn[0])]
    cross_all = gather(both_cross)
    feed = [gather(layer_feed[0])]
    attn.append(gather(layer_attn[1]))
    feed.append(gather(layer_feed[1]))
    cross_full = jnp.concatenate([cross_all[:, :cross_width], cross_all[:, cross_width:]], 0)
    cross_query_w = cross_full[:, :width]
    cross_keys_w = cross_full[:, width : 3 * width]
    cross_out_w = cross_full[:, 3 * width : 4 * width]
    cross_gain_w = cross_full[:, 4 * width].astype(F32)
    cross_shift_w = cross_full[:, 4 * width + 1].astype(F32)

    def layer_weights(index):
        a, f = attn[index], feed[index]
        vectors = a[:, 3 * half + width :].astype(F32).T
        bias = vectors[5:].reshape(half_ff)
        down = jnp.concatenate([f[:, half_ff + i * width : half_ff + (i + 1) * width] for i in range(folds)], 0)
        return dict(
            into=a[:, : 3 * half], out=a[:, 3 * half : 3 * half + width], up=f[:, :half_ff], down=down,
            self_gain=vectors[0], self_shift=vectors[1], feed_gain=vectors[2], feed_shift=vectors[3],
            down_bias=vectors[4], up_bias=bias,
        )

    place = jnp.arange(slots)
    keep = ((place[None, :] <= place[:, None])[None] & (place[None, None, :] < lengths[:, None, None]))[:, None]

    whole_text = side(text, swap(text), section, 1)
    whole_cot = side(cotangent, swap(cotangent), section, 1)

    def self_forward(inputs, w):
        normed = norm(inputs, w["self_gain"], w["self_shift"])
        projected = low(dot(normed, w["into"]))
        queries, keys, values = (split_heads(projected[:, i * half : (i + 1) * half], captions) for i in range(3))
        scores = jnp.where(keep, scores_of(queries, keys), MASKED)
        chances = softmax_rows(scores)
        mixed = low(mix(low(chances), values)).reshape(rows, half)
        mixed_all = side(mixed, swap(mixed), section, 1)
        current = inputs + dot(mixed_all, w["out"])
        return current, (normed, queries, keys, values, chances, mixed_all)

    def feed_forward(current, w):
        normed = norm(current, w["feed_gain"], w["feed_shift"])
        raised = dot(normed, w["up"]) + w["up_bias"]
        active = low(gelu(raised))
        part = low(dot(active, w["down"]))
        return part, (normed, raised, active)

    w0, w1 = layer_weights(0), layer_weights(1)
    flat_image = image.reshape(captions * half_image, width)
    pairs = low(dot(flat_image, cross_keys_w))
    image_keys = split_heads(pairs[:, :width], captions)
    image_values = split_heads(pairs[:, width:], captions)

    text32 = whole_text.astype(F32)
    mid_0, saved_0 = self_forward(text32, w0)
    part_0, feed_saved_0 = feed_forward(mid_0, w0)
    hidden = low(mid_0 + (part_0.astype(F32) + swap(part_0).astype(F32)) + w0["down_bias"]).astype(F32)

    first_1, saved_1 = self_forward(hidden, w1)
    cross_normed = norm(first_1, cross_gain_w, cross_shift_w)
    cross_queries = split_heads(low(dot(cross_normed, cross_query_w)), captions)
    cross_scores = scores_of(cross_queries, image_keys)
    top = jnp.max(cross_scores, -1, keepdims=True)
    raised_scores = jnp.exp(cross_scores - top)
    total = jnp.sum(raised_scores, -1, keepdims=True)
    part_mix = low(mix(low(raised_scores), image_values))
    stats = jnp.concatenate([top, total], -1)
    other_mix, other_stats = swap(part_mix), swap(stats)
    best = jnp.maximum(top, other_stats[..., :1])
    own_weight = jnp.exp(top - best)
    other_weight = jnp.exp(other_stats[..., :1] - best)
    inverse = 1.0 / (total * own_weight + other_stats[..., 1:] * other_weight)
    own_factor, other_factor = own_weight * inverse, other_weight * inverse
    flip = lambda v: v.transpose(0, 2, 1, 3)
    cross_mixed = flip(own_factor) * part_mix.astype(F32) + flip(other_factor) * other_mix.astype(F32)
    cross_chances = raised_scores * own_factor
    cross_mixed_low = low(cross_mixed).reshape(rows, width)
    mid_1 = first_1 + dot(cross_mixed_low, cross_out_w)
    part_1, feed_saved_1 = feed_forward(mid_1, w1)
    own_part = pick(section, part_1[:, :half], part_1[:, half:])
    got_part = swap(pick(section, part_1[:, half:], part_1[:, :half]))
    own_cols = lambda v: pick(section, v[..., :half], v[..., half:])
    layer_out = own_cols(mid_1) + own_part.astype(F32) + got_part.astype(F32) + own_cols(w1["down_bias"])

    def feed_back(grad, current, saved, w):
        normed, raised, active = saved
        grad_low = low(grad)
        down_grad = dot_tn(active, grad_low)
        grad_raised = low(dot_nt(grad_low, w["down"]) * gelu_slope(raised))
        up_grad = dot_tn(normed, grad_raised)
        bias_grad = jnp.sum(grad_raised.astype(F32), 0)
        part = low(dot_nt(grad_raised, w["up"]))
        inner = part.astype(F32) + swap(part).astype(F32)
        step, gain_grad, shift_grad = norm_back(current, w["feed_gain"], inner)
        down_cols = jnp.concatenate([down_grad[i * width : (i + 1) * width] for i in range(folds)], 1)
        return step + grad, low(jnp.concatenate([up_grad, down_cols], 1)), (gain_grad, shift_grad, jnp.sum(grad, 0), bias_grad)

    def self_back(grad, inputs, saved, w):
        normed, queries, keys, values, chances, mixed_all = saved
        grad_low = low(grad)
        out_rows = pick(section, w["out"][:half], w["out"][half:])
        grad_mixed = split_heads(low(dot_nt(grad_low, out_rows)), captions)
        grad_chances = jnp.einsum("cqhd,ckhd->chqk", grad_mixed, values, preferred_element_type=F32)
        slope = chances * (grad_chances - jnp.sum(grad_chances * chances, -1, keepdims=True))
        query_part, key_part = attend_back(queries, keys, values, chances, slope)
        value_part = jnp.einsum("chqk,cqhd->ckhd", low(chances), grad_mixed, preferred_element_type=F32)
        grad_projected = low(jnp.concatenate([v.reshape(rows, half) for v in (query_part, key_part, value_part)], 1))
        into_grad = low(dot_tn(normed, grad_projected))
        part = low(dot_nt(grad_projected, w["into"]))
        inner = part.astype(F32) + swap(part).astype(F32)
        step, gain_grad, shift_grad = norm_back(inputs, w["self_gain"], inner)
        return step + grad, into_grad, grad_low, (gain_grad, shift_grad)

    def scatter(value):
        return lax.psum_scatter(value, "dp", scatter_dimension=0, tiled=True)

    cot32 = whole_cot.astype(F32)
    grad_mid_1, feed_grad_1, feed_vec_1 = feed_back(cot32, mid_1, feed_saved_1, w1)
    feed_got_1 = scatter(feed_grad_1)
    branch_low = low(grad_mid_1)
    own_mixed = own_cols(cross_mixed_low)
    cross_out_grad = dot_tn(own_mixed, branch_low)
    grad_mixed_flat = low(dot_nt(branch_low, cross_out_w))
    grad_mixed = split_heads(grad_mixed_flat, captions)
    grad_chances = jnp.einsum("cqhd,ckhd->chqk", grad_mixed, image_values, preferred_element_type=F32)
    delta = flip(jnp.sum(grad_mixed.astype(F32) * cross_mixed, -1, keepdims=True))
    slope = cross_chances * (grad_chances - delta)
    query_part, key_part = attend_back(cross_queries, image_keys, image_values, cross_chances, slope)
    value_part = jnp.einsum("chqk,cqhd->ckhd", low(cross_chances), grad_mixed, preferred_element_type=F32)
    query_low = low(query_part.reshape(rows, width))
    grad_queries = low(query_low.astype(F32) + swap(query_low).astype(F32))
    grad_pairs = low(jnp.concatenate([key_part.reshape(-1, width), value_part.reshape(-1, width)], 1))
    image_grad = dot_nt(grad_pairs, cross_keys_w).reshape(captions, half_image, width)
    keys_grad = dot_tn(flat_image, grad_pairs)
    keys_cols = jnp.concatenate([keys_grad[:half], keys_grad[half:]], 1)
    query_grad = dot_tn(own_cols(cross_normed), grad_queries)
    step, cross_gain_grad, cross_shift_grad = norm_back(first_1, cross_gain_w, dot_nt(grad_queries, cross_query_w))
    grad_first_1 = step + grad_mid_1
    cross_vec = jnp.stack([own_cols(cross_gain_grad), own_cols(cross_shift_grad)], 1)
    cross_got = scatter(low(jnp.concatenate([query_grad, cross_out_grad, keys_cols, cross_vec], 1)))

    grad_hidden, into_grad_1, g_low_1, self_vec_1 = self_back(grad_first_1, hidden, saved_1, w1)
    into_got_1 = scatter(into_grad_1)
    grad_mid_0, feed_grad_0, feed_vec_0 = feed_back(grad_hidden, mid_0, feed_saved_0, w0)
    feed_got_0 = scatter(feed_grad_0)
    text_grad, into_grad_0, g_low_0, self_vec_0 = self_back(grad_mid_0, text32, saved_0, w0)
    out_grad = dot_tn(pick(section, saved_0[5], saved_1[5]), pick(section, g_low_0, g_low_1))
    own_vec = [pick(section, a, b) for a, b in zip(self_vec_0 + feed_vec_0[:3], self_vec_1 + feed_vec_1[:3])]
    bias_cols = [v[3].reshape(folds, width)[i] for v in (feed_vec_0, feed_vec_1) for i in range(folds)]
    last_got = scatter(low(jnp.concatenate([into_grad_0, out_grad, jnp.stack(own_vec + bias_cols, 1)], 1)))
    into_got_0 = last_got[:, : 3 * half]
    out_got = last_got[:, 3 * half : 3 * half + width]
    vec_got = last_got[:, 3 * half + width :]
    bias_got = [vec_got[:, 5 + folds * l : 5 + folds * (l + 1)] for l in range(2)]

    def from_both(first, later):
        got = swap(pick(section, later, first))
        own = pick(section, first, later)
        return pick(section, own, got).astype(F32), pick(section, got, own).astype(F32)

    into_parts = from_both(into_got_0, into_got_1)
    feed_parts = from_both(feed_got_0, feed_got_1)
    bias_parts = from_both(*bias_got)
    heads_in_grad = jnp.stack([v.reshape(piece, 3, half) for v in into_parts], 2).reshape(1, piece, 6 * half)
    up_parts = [v[:, :half_ff].reshape(piece, folds, count, piece).transpose(0, 2, 1, 3) for v in feed_parts]
    up_grad = jnp.stack(up_parts, 2).reshape(1, piece, 2 * half_ff)
    down_parts = [v[:, half_ff:].reshape(piece, folds, width).transpose(1, 0, 2) for v in feed_parts]
    down_grad = jnp.stack(down_parts, 0).reshape(1, 2 * folds * piece, width)
    up_bias_grad = jnp.stack([v.T for v in bias_parts], 0).reshape(1, 2 * folds * piece)
    vec32 = vec_got.astype(F32).T
    keys_got = cross_got[:, 2 * width : 6 * width]
    pair_width = 2 * width
    own_keys = pick(section, keys_got[:, :pair_width], keys_got[:, pair_width:])
    got_keys = swap(pick(section, keys_got[:, pair_width:], keys_got[:, :pair_width]))
    cross32 = cross_got.astype(F32)
    return (
        layer_out,
        own_cols(text_grad),
        image_grad,
        vec32[0][None],
        vec32[1][None],
        heads_in_grad,
        out_got.astype(F32)[None],
        vec32[2][None],
        vec32[3][None],
        up_grad,
        up_bias_grad,
        down_grad,
        vec32[4][None],
        cross32[:, 6 * width],
        cross32[:, 6 * width + 1],
        cross32[:, :width],
        own_keys.astype(F32) + got_keys.astype(F32),
        cross32[:, width : 2 * width],
    )


def solution(mesh):
    placed = (
        P("dp", "section"),
        P("dp", "section", None),
        P("dp"),
        P("section", "dp"),
        P("section", "dp"),
        P("section", "dp", None),
        P("section", "dp", None),
        P("section", "dp"),
        P("section", "dp"),
        P("section", "dp", None),
        P("section", "dp"),
        P("section", "dp", None),
        P("section", "dp"),
        P(("section", "dp")),
        P(("section", "dp")),
        P(("section", "dp"), None),
        P(("section", "dp"), None),
        P(("section", "dp"), None),
        P("dp", "section"),
    )
    return jax.shard_map(
        body,
        mesh=mesh,
        in_specs=placed,
        out_specs=(P("dp", "section"), P("dp", "section"), P("dp", "section", None)) + placed[3:18],
        check_vma=False,
    )
```

time: 2200 us -> 865 us (0.39)
  waiting for transfers between devices: 1390 us -> 473 us
  blocking collectives: 140 us -> 0 us
  matrix products: 219 us -> 100 us
  local copies, waits for them, and re-layouts: 255 us -> 184 us
  starting transfers between devices: 82.6 us -> 29.6 us
    reduce_scatter x7 -> x4, waiting for transfers between devices: 696 us -> 264 us  [scatter(): return lax.psum_scatter(value, 'dp', scatter_dimension=0, tiled=True)]
    ppermute x8 -> x20, waiting for transfers between devices: 327 us -> 58.8 us  [swap(): return lax.ppermute(value, 'section', [(0, 1), (1, 0)])]
    unnamed x3 -> x0, blocking collectives: 140 us -> none
    dot_general x72 -> x50, matrix products: 219 us -> 100 us  [the longest x11 25.5 us: dot(): return jnp.dot(left, right, preferred_element_type=F32)]
    unnamed x26 -> x11, waiting for transfers between devices: 121 us -> 3.96 us
    all_gather x7 -> x5, waiting for transfers between devices: 242 us -> 146 us  [gather(): return lax.all_gather(value, 'dp', axis=0, tiled=True)]
    convert_element_type x24 -> x3, local copies, waits for them, and re-layouts: 53 us -> 5.13 us  [low(): return values.astype(BF16)]
    ppermute x8 -> x20, starting transfers between devices: 72.7 us -> 28.7 us  [swap(): return lax.ppermute(value, 'section', [(0, 1), (1, 0)])]
  transfers between devices with their start and end apart: 30 -> 30, of which waited for: 19 -> 23; matrix products, arithmetic and copies ran while one was open for 12% -> 26% of each run, Pallas kernels for 0% -> 0%
where the time goes in v1:
time: 865 us; the launch traced here: 857 us
  waiting for transfers between devices  473 us (55%)
  local copies, waits for them, and re-layouts  184 us (21%)
  matrix products  100 us (12%)
  other arithmetic  51.7 us (6%)
  starting transfers between devices  29.6 us (3%)
  between operations  17.9 us (2%)
    reduce_scatter x4, waiting for transfers between devices, scatter(): return lax.psum_scatter(value, 'dp', scatter_dimension=0, tiled=True)  264 us
    all_gather x5, waiting for transfers between devices, gather(): return lax.all_gather(value, 'dp', axis=0, tiled=True)  146 us
    ppermute x20, waiting for transfers between devices, swap(): return lax.ppermute(value, 'section', [(0, 1), (1, 0)])  58.8 us
    reshape x20, local copies, waits for them, and re-layouts, split_heads(): values.reshape(captions, rows // captions, width // HEAD_DIM, HEAD_DIM)  34.6 us
    ppermute x20, starting transfers between devices, swap(): return lax.ppermute(value, 'section', [(0, 1), (1, 0)])  28.7 us
    unnamed x344, local copies, waits for them, and re-layouts  28.6 us
    dot_general x11, matrix products, dot(): return jnp.dot(left, right, preferred_element_type=F32)  25.5 us
    dot_general x11, matrix products, dot_nt(): lax.dot_general(left, right, (((1,), (1,)), ((), ())), preferred_element_...  24.3 us
  transfers between devices with their start and end apart: 30, of which 23 were waited for; matrix products, arithmetic and copies ran while one was open for 26% of the time, Pallas kernels for 0%

profile of v1, /device:TPU:0, one launch (start us, length us, event | category | flops | bytes accessed | tf_op | source)
XLA Modules:
  0.0 857.0 jit_solution(15592402734053334999)
XLA Ops:
  16.0 3.0 collective-permute-start.1
  19.0 4.9 collective-permute-done.1
  27.6 3.5 collective-permute-done.6
  36.8 5.3 collective-permute-done.3
  45.4 4.0 collective-permute-done
  53.8 17.7 %all-gather.6.cloned.1.call-done = bf16[768,1927]{1,0:T(8,128)(2,1)} async-done(((bf16[48,1927]{1,0:T(8,128)(2,1)}), bf16[768,1927]{1,0:T(8,128)(2,1)}) %all-gather.6.cloned.1.call-update) | async-done | bytes 2959888 | tf_op jit(solution)/shard_map/all_gather | solution.py:150
  74.1 2.3 convolution_convert_fusion.9
  77.8 2.2 reshape.486
  92.2 26.2 %all-gather.10.cloned.1.call-done = bf16[768,1927]{1,0:T(8,128)(2,1)} async-done(((bf16[48,1927]{1,0:T(8,128)(2,1)}), bf16[768,1927]{1,0:T(8,128)(2,1)}) %all-gather.10.cloned.1.call-update) | async-done | bytes 2959888 | tf_op jit(solution)/shard_map/all_gather | solution.py:150
  125.2 48.7 %all-gather.12.cloned.1.call-done = bf16[384,6148]{1,0:T(8,128)(2,1)} async-done(((bf16[24,6148]{1,0:T(8,128)(2,1)}), bf16[384,6148]{1,0:T(8,128)(2,1)}) %all-gather.12.cloned.1.call-update) | async-done | bytes 4721680 | tf_op jit(solution)/shard_map/all_gather | solution.py:150
  173.9 5.6 fusion.188
  179.6 6.7 fusion.2
  186.3 42.4 %all-gather.8.cloned.1.call-done = bf16[768,3072]{1,0:T(8,128)(2,1)} async-done(((bf16[48,3072]{1,0:T(8,128)(2,1)}), bf16[768,3072]{1,0:T(8,128)(2,1)}) %all-gather.8.cloned.1.call-update) | async-done | bytes 4718608 | tf_op jit(solution)/shard_map/all_gather | solution.py:150
  232.1 2.2 multiply_convert_fusion.8
  236.9 2.1 fusion.191
  238.9 5.6 reshape.435
  244.6 5.6 reshape.434
  251.5 3.3 pad_maximum_fusion.14
  271.5 11.2 %all-gather.14.cloned.1.call-done = bf16[768,3072]{1,0:T(8,128)(2,1)} async-done(((bf16[48,3072]{1,0:T(8,128)(2,1)}), bf16[768,3072]{1,0:T(8,128)(2,1)}) %all-gather.14.cloned.1.call-update) | async-done | bytes 4718608 | tf_op jit(solution)/shard_map/all_gather | solution.py:150
  282.8 3.3 fusion.189
  293.9 2.9 multiply_reduce_fusion
  304.1 17.5 %collective-permute-done.8 = bf16[4,64,12,64]{1,3,2,0:T(8,128)(2,1)S(1)} collective-permute-done((bf16[4,64,12,64]{1,3,2,0:T(8,128)(2,1)S(1)}, bf16[4,64,12,64]{1,3,2,0:T(8,128)(2,1)S(1)}, u32[]{:S(2)}, u32[]{:S(2)}) %collective-permute-start.8) | collective-permute-done | bytes 393248 | tf_op jit(solution)/shard_map/ppermute | solution.py:15
  323.7 2.1 fusion.210
  326.1 3.6 multiply_convert_fusion.7
  339.9 3.3 collective-permute-done.11
  343.2 2.1 multiply_reduce_fusion.3
  345.4 2.3 convert_reduce_fusion.2
  350.7 2.5 copy.519
  353.2 5.5 convert_bitcast_fusion
  360.5 2.7 multiply_convert_fusion.1
  365.0 2.2 fusion.7
  368.4 2.1 copy.576
  370.6 4.9 copy.551
  375.5 4.7 reshape.446
  380.1 2.6 copy.521
  384.7 5.0 copy.553
  389.7 4.6 reshape.447
  397.8 3.6 fusion.3
  408.3 2.5 fusion.82
  415.7 3.2 fusion.71
  423.1 15.6 %concatenate.90 = bf16[384,4610]{0,1:T(8,128)(2,1)} concatenate(bf16[384,768]{0,1:T(8,128)(2,1)S(1)} %copy.575, bf16[384,768]{0,1:T(8,128)(2,1)} %copy.576, bf16[384,1536]{0,1:T(8,128)(2,1)} %get-tuple-element.162, bf16[384,1536]{0,1:T(8,128)(2,1)S(1)} %copy-done.33, bf16[384,1]{0,1:T(2,128)(2,1)S(1)} %stack.57, bf16[384,1]{0,1:T(2,128)(2,1)S(1)} %stack.58), dimensions={1} | concatenate | bytes 7080960 | tf_op jit(solution)/shard_map/concatenate | solution.py:291
  439.7 2.1 fusion.108
  443.6 3.0 fusion.211
  450.5 5.2 collective-permute-done.14
  461.3 2.6 fusion.83
  483.5 2.5 fusion.68
  487.1 2.1 convolution_convert_fusion.7
  496.4 6.9 concatenate.87
  504.0 3.1 convolution_convert_fusion.6
  511.4 2.5 pad_maximum_fusion.1
  513.9 2.3 convolution_convert_fusion.4
  518.4 2.8 pad_maximum_fusion
  522.3 2.4 fusion.67
  527.2 3.3 collective-permute-done.9
  531.4 7.6 fusion.146
  540.1 3.1 all-reduce.3.cloned.1.call-done
  546.6 2.1 dynamic-slice_convert_fusion
  550.7 4.1 collective-permute-done.19
  557.7 55.2 %reduce-scatter.6.cloned.1.call-done = bf16[48,1929]{1,0:T(8,128)(2,1)} async-done(((bf16[768,1929]{1,0:T(8,128)(2,1)}), bf16[48,1929]{1,0:T(8,128)(2,1)}) %reduce-scatter.6.cloned.1.call-update) | async-done | bytes 185200 | tf_op jit(solution)/shard_map/reduce_scatter | solution.py:266
  620.0 56.4 %reduce-scatter.8.cloned.1.call-done = bf16[48,1152]{1,0:T(8,128)(2,1)} async-done(((bf16[768,1152]{1,0:T(8,128)(2,1)}), bf16[48,1152]{1,0:T(8,128)(2,1)}) %reduce-scatter.8.cloned.1.call-update) | async-done | bytes 110608 | tf_op jit(solution)/shard_map/reduce_scatter | solution.py:266
  681.1 74.2 %reduce-scatter.12.cloned.1.call-done = bf16[48,3072]{1,0:T(8,128)(2,1)} async-done(((bf16[768,3072]{1,0:T(8,128)(2,1)}), bf16[48,3072]{1,0:T(8,128)(2,1)}) %reduce-scatter.12.cloned.1.call-update) | async-done | bytes 294928 | tf_op jit(solution)/shard_map/reduce_scatter | solution.py:266
  755.3 78.3 %reduce-scatter.10.cloned.1.call-done = bf16[48,3072]{1,0:T(8,128)(2,1)} async-done(((bf16[768,3072]{1,0:T(8,128)(2,1)}), bf16[48,3072]{1,0:T(8,128)(2,1)}) %reduce-scatter.10.cloned.1.call-update) | async-done | bytes 294928 | tf_op jit(solution)/shard_map/reduce_scatter | solution.py:266
  838.7 3.8 collective-permute-done.17
  846.6 3.2 reshape.453
  (619 shorter events, 208.7 us)
Async XLA Ops:
  7.2 172.4 %copy-start = (bf16[4,288,768]{2,1,0:T(8,128)(2,1)S(1)}, bf16[4,288,768]{2,1,0:T(8,128)(2,1)}, u32[]{:S(2)}) copy-start(bf16[4,288,768]{2,1,0:T(8,128)(2,1)} %param.20) | copy-start | bytes 5308420
  7.2 64.3 %all-gather.6.cloned.1.call-start = ((), (), s32[]{:S(2)}) async-start(), calls=%async_computation.4 | async-start | bytes 3342336 | tf_op jit(solution)/shard_map/all_gather | solution.py:150
  9.8 15.7 %copy-start.149 = (bf16[24]{0:T(256)(128)(2,1)S(1)}, bf16[24]{0:T(256)(128)(2,1)}, u32[]{:S(2)}) copy-start(bf16[24]{0:T(256)(128)(2,1)} %param.32) | copy-start | bytes 148
  9.8 15.8 %copy-start.150 = (bf16[24]{0:T(256)(128)(2,1)S(1)}, bf16[24]{0:T(256)(128)(2,1)}, u32[]{:S(2)}) copy-start(bf16[24]{0:T(256)(128)(2,1)} %param.33) | copy-start | bytes 148
  10.6 15.1 %copy-start.100 = (bf16[24,1536]{1,0:T(8,128)(2,1)S(1)}, bf16[24,1536]{1,0:T(8,128)(2,1)}, u32[]{:S(2)}) copy-start(bf16[24,1536]{1,0:T(8,128)(2,1)} %param.35) | copy-start | bytes 221188
  10.6 15.1 %copy-start.114 = (bf16[24,768]{1,0:T(8,128)(2,1)S(1)}, bf16[24,768]{1,0:T(8,128)(2,1)}, u32[]{:S(2)}) copy-start(bf16[24,768]{1,0:T(8,128)(2,1)} %param.34) | copy-start | bytes 110596
  10.6 15.1 %copy-start.115 = (bf16[24,768]{1,0:T(8,128)(2,1)S(1)}, bf16[24,768]{1,0:T(8,128)(2,1)}, u32[]{:S(2)}) copy-start(bf16[24,768]{1,0:T(8,128)(2,1)} %param.36) | copy-start | bytes 110596
  14.8 17.2 %copy-start.97 = (bf16[1,192,768]{2,1,0:T(8,128)(2,1)S(1)}, bf16[1,192,768]{2,1,0:T(8,128)(2,1)}, u32[]{:S(2)}) copy-start(bf16[1,192,768]{2,1,0:T(8,128)(2,1)} %param.30) | copy-start | bytes 884740
  16.0 16.3 %copy-start.98 = (bf16[1,48,3072]{2,1,0:T(8,128)(2,1)S(1)}, bf16[1,48,3072]{2,1,0:T(8,128)(2,1)}, u32[]{:S(2)}) copy-start(bf16[1,48,3072]{2,1,0:T(8,128)(2,1)} %param.28) | copy-start | bytes 884740
  16.0 7.9 collective-permute-start.1
  24.7 93.7 %all-gather.10.cloned.1.call-start = ((), (), s32[]{:S(2)}) async-start(), calls=%async_computation.6 | async-start | bytes 3342336 | tf_op jit(solution)/shard_map/all_gather | solution.py:150
  25.4 148.5 %all-gather.12.cloned.1.call-start = ((), (), s32[]{:S(2)}) async-start(), calls=%async_computation.7 | async-start | bytes 5117952 | tf_op jit(solution)/shard_map/all_gather | solution.py:150
  25.8 5.2 collective-permute-start.6
  31.9 196.7 %all-gather.8.cloned.1.call-start = ((), (), s32[]{:S(2)}) async-start(), calls=%async_computation.5 | async-start | bytes 5013504 | tf_op jit(solution)/shard_map/all_gather | solution.py:150
  34.3 10.8 %copy-start.151 = (s32[4]{0:T(128)S(1)}, s32[4]{0:T(128)}, u32[]{:S(2)}) copy-start(s32[4]{0:T(128)} %param.21) | copy-start | bytes 52
  35.0 7.1 collective-permute-start.3
  43.0 239.8 %all-gather.14.cloned.1.call-start = ((), (), s32[]{:S(2)}) async-start(), calls=%async_computation.8 | async-start | bytes 5013504 | tf_op jit(solution)/shard_map/all_gather | solution.py:150
  43.1 6.3 collective-permute-start
  44.6 6.9 collective-permute-start.10
  49.4 73.5 %copy-start.26 = (bf16[256,384]{1,0:T(8,128)(2,1)}, bf16[256,384]{1,0:T(8,128)(2,1)S(1)}, u32[]{:S(2)}) copy-start(bf16[256,384]{1,0:T(8,128)(2,1)S(1)} %get-tuple-element.197) | copy-start | bytes 589828
  49.4 73.5 %copy-start.28 = (bf16[256,384]{1,0:T(8,128)(2,1)}, bf16[256,384]{1,0:T(8,128)(2,1)S(1)}, u32[]{:S(2)}) copy-start(bf16[256,384]{1,0:T(8,128)(2,1)S(1)} %get-tuple-element.198) | copy-start | bytes 589828
  49.6 26.8 %copy-start.128 = (f32[256]{0:T(256)}, f32[256]{0:T(256)S(1)}, u32[]{:S(2)}) copy-start(f32[256]{0:T(256)S(1)} %broadcast_multiply_fusion.14) | copy-start | bytes 3076
  49.9 26.5 %copy-start.139 = (f32[256]{0:T(256)}, f32[256]{0:T(256)S(1)}, u32[]{:S(2)}) copy-start(f32[256]{0:T(256)S(1)} %add_rsqrt_fusion.4) | copy-start | bytes 3076
  53.3 489.9 %all-reduce.3.cloned.1.call-start = ((), (), s32[]{:S(2)}) async-start(), calls=%async_computation.13 | async-start | bytes 7090176
  73.5 157.1 %copy-start.103 = (f32[768]{0:T(1024)}, f32[768]{0:T(1024)S(1)}, u32[]{:S(2)}) copy-start(f32[768]{0:T(1024)S(1)} %get-tuple-element.136) | copy-start | bytes 9220
  73.5 157.1 %copy-start.122 = (f32[768]{0:T(1024)}, f32[768]{0:T(1024)S(1)}, u32[]{:S(2)}) copy-start(f32[768]{0:T(1024)S(1)} %get-tuple-element.135) | copy-start | bytes 9220
  90.7 31.1 %collective-permute-start.2 = (bf16[256,384]{1,0:T(8,128)(2,1)}, bf16[256,384]{1,0:T(8,128)(2,1)}, u32[]{:S(2)}, u32[]{:S(2)}) collective-permute-start(bf16[256,384]{1,0:T(8,128)(2,1)} %reshape.469), channel_id=1, source_target_pairs={{0,16},{16,0},{1,17},{17,1},{2,18},{18,2},{3,19},{19,3},{4,20},{20... | collective-permute-start | bytes 589832 | tf_op jit(solution)/shard_map/ppermute | solution.py:15
  121.9 134.6 %copy-start.107 = (f32[768]{0:T(1024)}, f32[768]{0:T(1024)S(1)}, u32[]{:S(2)}) copy-start(f32[768]{0:T(1024)S(1)} %get-tuple-element.133) | copy-start | bytes 9220
  121.9 134.6 %copy-start.126 = (f32[768]{0:T(1024)}, f32[768]{0:T(1024)S(1)}, u32[]{:S(2)}) copy-start(f32[768]{0:T(1024)S(1)} %get-tuple-element.132) | copy-start | bytes 9220
  124.9 129.9 %copy-start.5 = (f32[256,768]{1,0:T(8,128)}, f32[256,768]{1,0:T(8,128)S(1)}, u32[]{:S(2)}) copy-start(f32[256,768]{1,0:T(8,128)S(1)} %get-tuple-element.223) | copy-start | bytes 2359300
  125.0 105.6 %copy-start.116 = (f32[256]{0:T(256)}, f32[256]{0:T(256)S(1)}, u32[]{:S(2)}) copy-start(f32[256]{0:T(256)S(1)} %broadcast_multiply_fusion.13) | copy-start | bytes 3076
  125.2 105.4 %copy-start.130 = (f32[256]{0:T(256)}, f32[256]{0:T(256)S(1)}, u32[]{:S(2)}) copy-start(f32[256]{0:T(256)S(1)} %add_rsqrt_fusion.3) | copy-start | bytes 3076
  235.3 19.5 %collective-permute-start.4 = (bf16[256,768]{1,0:T(8,128)(2,1)S(1)}, bf16[256,768]{1,0:T(8,128)(2,1)}, u32[]{:S(2)}, u32[]{:S(2)}) collective-permute-start(bf16[256,768]{1,0:T(8,128)(2,1)S(1)} %fusion.66), channel_id=1, source_target_pairs={{0,16},{16,0},{1,17},{17,1},{2,18},{18,2},{3,19},{19,3},{4,20},{20... | collective-permute-start | bytes 1179656 | tf_op jit(solution)/shard_map/ppermute | solution.py:15
  251.5 36.9 %copy-start.112 = (f32[768]{0:T(1024)}, f32[768]{0:T(1024)S(1)}, u32[]{:S(2)}) copy-start(f32[768]{0:T(1024)S(1)} %get-tuple-element.108) | copy-start | bytes 9220
  256.1 30.0 %copy-start.15 = (bf16[256,768]{1,0:T(8,128)(2,1)}, bf16[256,768]{1,0:T(8,128)(2,1)S(1)}, u32[]{:S(2)}) copy-start(bf16[256,768]{1,0:T(8,128)(2,1)S(1)} %get-tuple-element.146) | copy-start | bytes 1179652
  270.1 15.9 %collective-permute-start.5 = (bf16[256,384]{1,0:T(8,128)(2,1)S(1)}, bf16[256,384]{1,0:T(8,128)(2,1)S(1)}, u32[]{:S(2)}, u32[]{:S(2)}) collective-permute-start(bf16[256,384]{1,0:T(8,128)(2,1)S(1)} %reshape.470), channel_id=1, source_target_pairs={{0,16},{16,0},{1,17},{17,1},{2,18},{18,2},{3,19},{19,3},{4,20},{20... | collective-permute-start | bytes 589832 | tf_op jit(solution)/shard_map/ppermute | solution.py:15
  298.2 5.2 collective-permute-start.7
  301.9 19.8 %copy-start.24 = (bf16[4,64,12,64]{1,3,2,0:T(8,128)(2,1)}, bf16[4,64,12,64]{1,3,2,0:T(8,128)(2,1)S(1)}, u32[]{:S(2)}) copy-start(bf16[4,64,12,64]{1,3,2,0:T(8,128)(2,1)S(1)} %fusion.53) | copy-start | bytes 1179652
  301.9 19.8 %collective-permute-start.8 = (bf16[4,64,12,64]{1,3,2,0:T(8,128)(2,1)S(1)}, bf16[4,64,12,64]{1,3,2,0:T(8,128)(2,1)S(1)}, u32[]{:S(2)}, u32[]{:S(2)}) collective-permute-start(bf16[4,64,12,64]{1,3,2,0:T(8,128)(2,1)S(1)} %fusion.53), channel_id=1, source_target_pairs={{0,16},{16,0},{1,17},{17,1},{2,18},{18,2},{3,19},{19,3},{4,20},{20... | collective-permute-start | bytes 1179656 | tf_op jit(solution)/shard_map/ppermute | solution.py:15
  304.1 18.0 %copy-start.93 = (f32[4,64,12]{1,2,0:T(8,128)}, f32[4,64,12]{1,2,0:T(8,128)S(1)}, u32[]{:S(2)}) copy-start(f32[4,64,12]{1,2,0:T(8,128)S(1)} %get-tuple-element.206) | copy-start | bytes 36868
  325.8 19.6 %copy-start.120 = (f32[256]{0:T(256)}, f32[256]{0:T(256)S(1)}, u32[]{:S(2)}) copy-start(f32[256]{0:T(256)S(1)} %broadcast_multiply_fusion.10) | copy-start | bytes 3076
  326.0 19.3 %copy-start.134 = (f32[256]{0:T(256)}, f32[256]{0:T(256)S(1)}, u32[]{:S(2)}) copy-start(f32[256]{0:T(256)S(1)} %add_rsqrt_fusion) | copy-start | bytes 3076
  332.4 10.8 %collective-permute-start.11 = (bf16[256,768]{1,0:T(8,128)(2,1)}, bf16[256,768]{1,0:T(8,128)(2,1)}, u32[]{:S(2)}, u32[]{:S(2)}) collective-permute-start(bf16[256,768]{1,0:T(8,128)(2,1)} %fusion.77), channel_id=1, source_target_pairs={{0,16},{16,0},{1,17},{17,1},{2,18},{18,2},{3,19},{19,3},{4,20},{20... | collective-permute-start | bytes 1179656 | tf_op jit(solution)/shard_map/ppermute | solution.py:15
  338.2 10.4 %copy-start.14 = (bf16[768,768]{1,0:T(8,128)(2,1)S(1)}, bf16[768,768]{1,0:T(8,128)(2,1)}, u32[]{:S(2)}) copy-start(bf16[768,768]{1,0:T(8,128)(2,1)} %get-tuple-element.147) | copy-start | bytes 3538948
  384.7 19.3 %copy-start.55 = (bf16[256,768]{0,1:T(8,128)(2,1)}, bf16[256,768]{0,1:T(8,128)(2,1)S(1)}, u32[]{:S(2)}) copy-start(bf16[256,768]{0,1:T(8,128)(2,1)S(1)} %convert_element_type.312) | copy-start | bytes 1179652
  394.4 9.5 %collective-permute-start.12 = (bf16[256,768]{0,1:T(8,128)(2,1)S(1)}, bf16[256,768]{0,1:T(8,128)(2,1)S(1)}, u32[]{:S(2)}, u32[]{:S(2)}) collective-permute-start(bf16[256,768]{0,1:T(8,128)(2,1)S(1)} %convert_element_type.312), channel_id=1, source_target_pairs={{0,16},{16,0},{1,17},{17,1},{2,18},{18,2},{3,19},{19,3},{4,20},{20... | collective-permute-start | bytes 1179656 | tf_op jit(solution)/shard_map/ppermute | solution.py:15
  419.0 19.9 %collective-permute-start.13 = (bf16[256,768]{1,0:T(8,128)(2,1)}, bf16[256,768]{1,0:T(8,128)(2,1)}, u32[]{:S(2)}, u32[]{:S(2)}) collective-permute-start(bf16[256,768]{1,0:T(8,128)(2,1)} %fusion.71), channel_id=1, source_target_pairs={{0,16},{16,0},{1,17},{17,1},{2,18},{18,2},{3,19},{19,3},{4,20},{20... | collective-permute-start | bytes 1179656 | tf_op jit(solution)/shard_map/ppermute | solution.py:15
  438.7 174.2 %reduce-scatter.6.cloned.1.call-start = ((), (), s32[]{:S(2)}) async-start(), calls=%async_computation.9 | async-start | bytes 3342336 | tf_op jit(solution)/shard_map/reduce_scatter | solution.py:266
  443.6 12.6 %copy-start.23 = (f32[256,768]{1,0:T(8,128)}, f32[256,768]{1,0:T(8,128)S(1)}, u32[]{:S(2)}) copy-start(f32[256,768]{1,0:T(8,128)S(1)} %get-tuple-element.142) | copy-start | bytes 2359300
  446.7 9.0 %copy-start.6 = (f32[256,768]{1,0:T(8,128)S(1)}, f32[256,768]{1,0:T(8,128)}, u32[]{:S(2)}) copy-start(f32[256,768]{1,0:T(8,128)} %copy-done.5) | copy-start | bytes 2359300
  446.7 9.0 %copy-start.104 = (f32[768]{0:T(1024)S(1)}, f32[768]{0:T(1024)}, u32[]{:S(2)}) copy-start(f32[768]{0:T(1024)} %copy-done.103) | copy-start | bytes 9220
  446.7 9.0 %copy-start.117 = (f32[256]{0:T(256)S(1)}, f32[256]{0:T(256)}, u32[]{:S(2)}) copy-start(f32[256]{0:T(256)} %copy-done.116) | copy-start | bytes 3076
  446.7 9.0 %copy-start.131 = (f32[256]{0:T(256)S(1)}, f32[256]{0:T(256)}, u32[]{:S(2)}) copy-start(f32[256]{0:T(256)} %copy-done.130) | copy-start | bytes 3076
  447.5 8.1 collective-permute-start.14
  486.1 7.8 collective-permute-start.15
  503.3 173.1 %reduce-scatter.8.cloned.1.call-start = ((), (), s32[]{:S(2)}) async-start(), calls=%async_computation.10 | async-start | bytes 1880064 | tf_op jit(solution)/shard_map/reduce_scatter | solution.py:266
  507.1 248.2 %reduce-scatter.12.cloned.1.call-start = ((), (), s32[]{:S(2)}) async-start(), calls=%async_computation.12 | async-start | bytes 5013504 | tf_op jit(solution)/shard_map/reduce_scatter | solution.py:266
  513.9 319.8 %reduce-scatter.10.cloned.1.call-start = ((), (), s32[]{:S(2)}) async-start(), calls=%async_computation.11 | async-start | bytes 5013504 | tf_op jit(solution)/shard_map/reduce_scatter | solution.py:266
  524.8 5.7 collective-permute-start.9
  545.1 9.7 %collective-permute-start.19 = (bf16[24,1536]{0,1:T(8,128)(2,1)S(1)}, bf16[24,1536]{0,1:T(8,128)(2,1)S(1)}, u32[]{:S(2)}, u32[]{:S(2)}) collective-permute-start(bf16[24,1536]{0,1:T(8,128)(2,1)S(1)} %broadcast_select_fusion), channel_id=1, source_target_pairs={{0,16},{16,0},{1,17},{17,1},{2,18},{18,2},{3,19},{19,3},{4,20},{20... | collective-permute-start | bytes 221192 | tf_op jit(solution)/shard_map/ppermute | solution.py:15
  613.8 65.6 %collective-permute-start.18 = (bf16[48,2]{1,0:T(8,128)(2,1)S(1)}, bf16[48,2]{1,0:T(8,128)(2,1)S(1)}, u32[]{:S(2)}, u32[]{:S(2)}) collective-permute-start(bf16[48,2]{1,0:T(8,128)(2,1)S(1)} %broadcast_select_fusion.26), channel_id=1, source_target_pairs={{0,16},{16,0},{1,17},{17,1},{2,18},{18,2},{3,19},{19,3},{4,20},{20... | collective-permute-start | bytes 584 | tf_op jit(solution)/shard_map/ppermute | solution.py:15
  678.0 158.2 %collective-permute-start.16 = (bf16[48,1152]{1,0:T(8,128)(2,1)S(1)}, bf16[48,1152]{1,0:T(8,128)(2,1)S(1)}, u32[]{:S(2)}, u32[]{:S(2)}) collective-permute-start(bf16[48,1152]{1,0:T(8,128)(2,1)S(1)} %broadcast_select_fusion.24), channel_id=1, source_target_pairs={{0,16},{16,0},{1,17},{17,1},{2,18},{18,2},{3,19},{19,3},{4,20},{20... | collective-permute-start | bytes 331784 | tf_op jit(solution)/shard_map/ppermute | solution.py:15
  755.3 87.1 %copy-start.61 = (bf16[48,3072]{1,0:T(8,128)(2,1)S(1)}, bf16[48,3072]{1,0:T(8,128)(2,1)}, u32[]{:S(2)}) copy-start(bf16[48,3072]{1,0:T(8,128)(2,1)} %reduce-scatter.12.cloned.1.call-done) | copy-start | bytes 884740
  834.7 7.7 collective-permute-start.17
  (126 other events, 430.4 us)
Sparse Core Ops, SparseCore 0:
  24.8 46.6 all-gather.5
  74.4 43.9 all-gather.9
  121.2 52.7 all-gather.11
  176.7 51.9 all-gather.7
  230.8 51.9 all-gather.13
  438.9 104.3 all-reduce.2
  547.5 65.4 reduce-scatter.5
  617.2 59.1 reduce-scatter.7
  680.8 74.5 reduce-scatter.11
  759.0 74.5 reduce-scatter.9

commit v2 on v1

v2 whole, which is shorter than its diff:
```python
import functools

import jax
import jax.numpy as jnp
from jax import lax
from jax.experimental import pallas as pl
from jax.experimental.pallas import tpu as pltpu
from jax.sharding import PartitionSpec as P

HEAD_DIM = 64
PAIR = 2 * HEAD_DIM
EPS = 1e-05
MASKED = -1000000000.0
SCALE = HEAD_DIM**-0.5
F32 = jnp.float32
BF16 = jnp.bfloat16
MIB = 1 << 20


def swap(value):
    return lax.ppermute(value, "section", [(0, 1), (1, 0)])


def pick(section, first, later):
    return jnp.where(section == 0, first, later)


def side(own, other, section, axis):
    return jnp.concatenate([pick(section, own, other), pick(section, other, own)], axis)


def low(values):
    return values.astype(BF16)


def ring_chip(place, chips):
    return jnp.where(place < chips // 2, 2 * place, 2 * (chips - 1 - place) + 1)


def ring_steps(shift):
    count = lax.axis_size("dp")
    chips = count // 2
    order = list(range(0, chips, 2)) + list(range(chips - 1, 0, -2))
    return [(2 * order[i] + core, 2 * order[(i + shift) % chips] + core) for i in range(chips) for core in range(2)]


def ring_move(value, shift):
    return lax.ppermute(value, "dp", ring_steps(shift))


def core_swap(value):
    return lax.ppermute(value, "dp", [(i, i ^ 1) for i in range(lax.axis_size("dp"))])


def my_place():
    chips = lax.axis_size("dp") // 2
    me = lax.axis_index("dp")
    chip, core = me // 2, me % 2
    return jnp.where(chip % 2 == 0, chip // 2, chips - 1 - chip // 2), core


def assemble_kernel(places, spots, *refs):
    *sources, out, sems = refs
    copies = []
    for i, (ref, index) in enumerate(places):
        source = sources[ref] if index is None else sources[ref].at[index]
        copies.append(pltpu.make_async_copy(source, out.at[spots[i]], sems.at[i]))
    for copy in copies:
        copy.start()
    for copy in copies:
        copy.wait()


def gather_kernel(chips, spots, *refs):
    assemble_kernel([(i, None) for i in range(chips)] + [(chips, i) for i in range(chips)], spots, *refs)


def ring_gather(shard):
    chips = lax.axis_size("dp") // 2
    half = chips // 2
    rows, width = shard.shape
    cut = rows // 2
    got = {0: shard}
    for step in range(1, half):
        got[-step] = ring_move(got[1 - step], 1)
        got[step] = ring_move(got[step - 1], -1)
    got[half] = jnp.concatenate([ring_move(got[1 - half][:cut], 1), ring_move(got[half - 1][cut:], -1)], 0)
    steps = list(range(1 - half, half + 1))
    mine = [got[step] for step in steps]
    other = core_swap(jnp.stack(mine))
    place, core = my_place()
    chip = [ring_chip((place + step + chips) % chips, chips) for step in steps]
    spots = jnp.stack([2 * c + core for c in chip] + [2 * c + 1 - core for c in chip]).astype(jnp.int32)
    out = pl.pallas_call(
        functools.partial(gather_kernel, chips),
        out_shape=jax.ShapeDtypeStruct((2 * chips, rows, width), shard.dtype),
        in_specs=[pl.BlockSpec(memory_space=pltpu.SMEM)] + [pl.BlockSpec(memory_space=pl.ANY)] * (chips + 1),
        out_specs=pl.BlockSpec(memory_space=pltpu.VMEM),
        scratch_shapes=[pltpu.SemaphoreType.DMA((2 * chips,))],
        compiler_params=pltpu.CompilerParams(vmem_limit_bytes=16 * MIB),
        cost_estimate=pl.CostEstimate(flops=0, bytes_accessed=4 * chips * rows * width * 2, transcendentals=0),
        name="assemble",
    )(spots, *mine, other)
    return out.reshape(2 * chips * rows, width)


def ring_scatter(value):
    chips = lax.axis_size("dp") // 2
    half = chips // 2
    total, width = value.shape
    rows = total // (2 * chips)
    cut = rows // 2
    parts = value.reshape(chips, 2, rows, width)
    place, core = my_place()
    mine = lax.dynamic_index_in_dim(parts, core, 1, False)
    got = core_swap(lax.dynamic_index_in_dim(parts, 1 - core, 1, False))

    def own(step, begin=0, end=rows):
        chip = ring_chip((place + step + chips) % chips, chips)
        cut_out = lambda v: lax.dynamic_index_in_dim(v, chip, 0, False)[begin:end].astype(F32)
        return cut_out(mine) + cut_out(got)

    up = ring_move(low(own(half, 0, cut)), 1)
    down = ring_move(low(own(-half, cut, rows)), -1)
    pad = jnp.zeros((cut, width), F32)
    up_all = jnp.concatenate([up.astype(F32), jnp.zeros((rows - cut, width), F32)], 0)
    down_all = jnp.concatenate([pad, down.astype(F32)], 0)
    for step in range(half - 1, 0, -1):
        up_all = ring_move(low(own(step) + up_all), 1).astype(F32)
        down_all = ring_move(low(own(-step) + down_all), -1).astype(F32)
    return own(0) + up_all + down_all


def norm_unit(values):
    centred = values - jnp.mean(values, -1, keepdims=True)
    scale = lax.rsqrt(jnp.mean(centred * centred, -1, keepdims=True) + EPS)
    return centred * scale, scale


def norm_back(values, gain, grad):
    unit, scale = norm_unit(values)
    wide = grad * gain
    inner = wide - jnp.mean(wide, -1, keepdims=True) - unit * jnp.mean(wide * unit, -1, keepdims=True)
    return inner * scale, jnp.sum(grad * unit, 0, keepdims=True), jnp.sum(grad, 0, keepdims=True)


def dot(left, right):
    return jnp.dot(left, right, preferred_element_type=F32)


def dot_tn(left, right):
    return lax.dot_general(left, right, (((0,), (0,)), ((), ())), preferred_element_type=F32)


def dot_nt(left, right):
    return lax.dot_general(left, right, (((1,), (1,)), ((), ())), preferred_element_type=F32)


def gelu(values):
    return 0.5 * values * (1.0 + lax.erf(values * 0.5**0.5))


def gelu_slope(values):
    return 0.5 * (1.0 + lax.erf(values * 0.5**0.5)) + values * jnp.exp(-0.5 * values * values) * 0.3989422804014327


def first_head(rows):
    return lax.broadcasted_iota(jnp.int32, (rows, PAIR), 1) < HEAD_DIM


def stacked(pair):
    mask = first_head(pair.shape[0])
    zero = jnp.zeros_like(pair)
    return jnp.concatenate([jnp.where(mask, pair, zero), jnp.where(mask, zero, pair)], 0)


def unstacked(rows):
    half = rows.shape[0] // 2
    return jnp.where(first_head(half), rows[:half], rows[half:])


def keep_mask(length, slots):
    query = lax.broadcasted_iota(jnp.int32, (2 * slots, slots), 0) % slots
    key = lax.broadcasted_iota(jnp.int32, (2 * slots, slots), 1)
    return (key <= query) & (key < length)


def self_chances(queries, keys, keep):
    scores = jnp.where(keep, dot_nt(queries, keys) * SCALE, MASKED)
    raised = jnp.exp(scores - jnp.max(scores, -1, keepdims=True))
    return raised / jnp.sum(raised, -1, keepdims=True)


def call(kernel, ins, outs, scratch=(), vmem=48, name=None, flops=0):
    specs, arrays = [], []
    for array, spec in ins:
        if spec is None:
            zeros = (0,) * array.ndim
            specs.append(pl.BlockSpec(array.shape, lambda i, z=zeros: z))
        elif spec == "s":
            specs.append(pl.BlockSpec(memory_space=pltpu.SMEM))
        else:
            block, index = spec
            specs.append(pl.BlockSpec(block, lambda i, z=index: z))
        arrays.append(array)
    shapes = [jax.ShapeDtypeStruct(*o) for o in outs]
    out_specs = [pl.BlockSpec(o.shape, lambda i, z=(0,) * len(o.shape): z) for o in shapes]
    moved = sum(a.size * a.dtype.itemsize for a in arrays) + sum(o.size * o.dtype.itemsize for o in shapes)
    return pl.pallas_call(
        kernel,
        grid=(1,),
        in_specs=specs,
        out_specs=out_specs,
        out_shape=shapes,
        scratch_shapes=list(scratch),
        compiler_params=pltpu.CompilerParams(vmem_limit_bytes=vmem * MIB),
        cost_estimate=pl.CostEstimate(flops=flops, bytes_accessed=moved, transcendentals=0),
        name=name,
    )(*arrays)


SELF_GAIN, SELF_SHIFT, FEED_GAIN, FEED_SHIFT, DOWN_BIAS, UP_BIAS = range(6)
LAYER_VECS = 7
CROSS_GAIN, CROSS_SHIFT = 14, 15


def vec(ref, row):
    return ref[row : row + 1, :]


def self_part(values, layer, lengths, vecs, wq, wk, wv, normed_ref, projected, mixed_ref):
    base = LAYER_VECS * layer
    unit, _ = norm_unit(values)
    normed = low(unit * vec(vecs, base + SELF_GAIN) + vec(vecs, base + SELF_SHIFT))
    normed_ref[...] = normed
    half = wq.shape[1]
    for i, weight in enumerate((wq, wk, wv)):
        projected[:, i * half : (i + 1) * half] = low(dot(normed, weight[...]))
    captions = lengths.shape[0]
    slots = values.shape[0] // captions
    for c in range(captions):
        keep = keep_mask(lengths[c], slots)
        here = slice(c * slots, (c + 1) * slots)
        for j in range(half // PAIR):
            q, k, v = (projected[here, i * half + j * PAIR : i * half + (j + 1) * PAIR] for i in range(3))
            chances = self_chances(stacked(q), k, keep)
            mixed_ref[here, j * PAIR : (j + 1) * PAIR] = low(unstacked(dot(low(chances), v)))


def self_first_kernel(lengths, text, vecs, wq, wk, wv, normed, projected, mixed):
    self_part(text[...].astype(F32), 0, lengths, vecs, wq, wk, wv, normed, projected, mixed)


def self_second_kernel(lengths, middle, own, other, vecs, wq, wk, wv, hidden, normed, projected, mixed):
    total = middle[...] + (own[...].astype(F32) + other[...].astype(F32)) + vec(vecs, DOWN_BIAS)
    hidden[...] = low(total)
    self_part(hidden[...].astype(F32), 1, lengths, vecs, wq, wk, wv, normed, projected, mixed)


def add_heads_out(values, section, own, other, out):
    half = own.shape[1]
    own_rows = pl.multiple_of(section * half, half)
    other_rows = pl.multiple_of((1 - section) * half, half)
    return values + (dot(own[...], out[pl.ds(own_rows, half), :]) + dot(other[...], out[pl.ds(other_rows, half), :]))


def feed_part(middle, layer, vecs, up, down, normed_ref, raised_ref, active_ref):
    base = LAYER_VECS * layer
    width = middle.shape[1]
    unit, _ = norm_unit(middle)
    normed = low(unit * vec(vecs, base + FEED_GAIN) + vec(vecs, base + FEED_SHIFT))
    normed_ref[...] = normed
    total = jnp.zeros_like(middle)
    for i in range(up.shape[1] // width):
        here = slice(i * width, (i + 1) * width)
        raised = dot(normed, up[:, here]) + vec(vecs, base + UP_BIAS + i)
        raised_ref[:, here] = raised
        active = low(gelu(raised))
        active_ref[:, here] = active
        total += dot(active, down[:, here])
    return low(total)


def feed_first_kernel(section, text, own, other, vecs, out, up, down, middle, normed, raised, active, part):
    values = add_heads_out(text[...].astype(F32), section[0], own, other, out)
    middle[...] = values
    part[...] = feed_part(values, 0, vecs, up, down, normed, raised, active)


def cross_kernel(section, hidden, own, other, vecs, out, query, pairs, first, normed_ref, queries, part, stats):
    values = add_heads_out(hidden[...].astype(F32), section[0], own, other, out)
    first[...] = values
    unit, _ = norm_unit(values)
    normed = low(unit * vec(vecs, CROSS_GAIN) + vec(vecs, CROSS_SHIFT))
    normed_ref[...] = normed
    queries[...] = low(dot(normed, query[...]))
    rows, width = values.shape
    captions = pairs.shape[0]
    slots = rows // captions
    lane = lax.broadcasted_iota(jnp.int32, (slots, PAIR), 1)

    def one(c, carry):
        here = pl.ds(pl.multiple_of(c * slots, slots), slots)
        record = jnp.zeros((slots, PAIR), F32)
        for j in range(width // PAIR):
            cols = slice(j * PAIR, (j + 1) * PAIR)
            k = pairs[c, :, cols]
            v = pairs[c, :, width + j * PAIR : width + (j + 1) * PAIR]
            scores = dot_nt(stacked(queries[here, cols]), k) * SCALE
            top = jnp.max(scores, -1, keepdims=True)
            raised = jnp.exp(scores - top)
            total = jnp.sum(raised, -1, keepdims=True)
            part[here, cols] = low(unstacked(dot(low(raised), v)))
            for i in range(2):
                block = slice(i * slots, (i + 1) * slots)
                record = jnp.where(lane == 2 * j + i, top[block], record)
                record = jnp.where(lane == HEAD_DIM + 2 * j + i, total[block], record)
        stats[here, :] = record
        return carry

    lax.fori_loop(0, captions, one, 0)


def feed_second_kernel(first, own, other, own_stats, other_stats, vecs, out, up, down, middle, mixed, factor, normed, raised, active, part):
    top, top_other = own_stats[...], other_stats[...]
    total, total_other = pltpu.roll(top, HEAD_DIM, 1), pltpu.roll(top_other, HEAD_DIM, 1)
    best = jnp.maximum(top, top_other)
    own_weight, other_weight = jnp.exp(top - best), jnp.exp(top_other - best)
    inverse = 1.0 / (total * own_weight + total_other * other_weight)
    own_factor, other_factor = own_weight * inverse, other_weight * inverse
    factor[...] = own_factor
    rows, width = first.shape
    mask = first_head(rows)
    for j in range(width // PAIR):
        cols = slice(j * PAIR, (j + 1) * PAIR)
        spread = lambda f: jnp.where(mask, f[:, 2 * j : 2 * j + 1], f[:, 2 * j + 1 : 2 * j + 2])
        mixed[:, cols] = low(spread(own_factor) * own[:, cols].astype(F32) + spread(other_factor) * other[:, cols].astype(F32))
    values = first[...] + dot(mixed[...], out[...])
    middle[...] = values
    part[...] = feed_part(values, 1, vecs, up, down, normed, raised, active)


def feed_back(grad, layer, vecs, up, down, raised, bias_grad, down_bias_grad, slope_ref, part):
    width = grad.shape[1]
    grad_low = low(grad)
    down_bias_grad[...] = jnp.sum(grad, 0, keepdims=True)
    total = jnp.zeros(grad.shape, F32)
    for i in range(up.shape[1] // width):
        here = slice(i * width, (i + 1) * width)
        grad_raised = low(dot_nt(grad_low, down[:, here]) * gelu_slope(raised[:, here]))
        slope_ref[:, here] = grad_raised
        bias_grad[i : i + 1, :] = jnp.sum(grad_raised.astype(F32), 0, keepdims=True)
        total += dot_nt(grad_raised, up[:, here])
    part[...] = low(total)


def feed_back_last_kernel(cot, vecs, up, down, raised, bias_grad, down_bias_grad, slope, part):
    feed_back(cot[...].astype(F32), 1, vecs, up, down, raised, bias_grad, down_bias_grad, slope, part)


def cross_back_kernel(cot, own, other, middle, vecs, out, queries, pairs, stats, factor, mixed, grad_ref, low_ref, vec_grad, query_part, grad_pairs, grad_mixed):
    base = LAYER_VECS
    inner = own[...].astype(F32) + other[...].astype(F32)
    step, gain_grad, shift_grad = norm_back(middle[...], vec(vecs, base + FEED_GAIN), inner)
    vec_grad[0:1, :] = gain_grad
    vec_grad[1:2, :] = shift_grad
    grad = step + cot[...].astype(F32)
    grad_ref[...] = grad
    low_ref[...] = low(grad)
    grad_mixed[...] = low(dot_nt(low_ref[...], out[...]))
    rows, width = grad.shape
    captions = pairs.shape[0]
    slots = rows // captions
    mask = first_head(slots)

    def one(c, carry):
        here = pl.ds(pl.multiple_of(c * slots, slots), slots)
        tops, factors = stats[here, :], factor[here, :]
        for j in range(width // PAIR):
            cols = slice(j * PAIR, (j + 1) * PAIR)
            later = slice(width + j * PAIR, width + (j + 1) * PAIR)
            k, v = pairs[c, :, cols], pairs[c, :, later]
            two = lambda a: jnp.concatenate([a[:, 2 * j : 2 * j + 1], a[:, 2 * j + 1 : 2 * j + 2]], 0)
            q = stacked(queries[here, cols])
            grad_pair = grad_mixed[here, cols]
            both = grad_pair.astype(F32) * mixed[here, cols].astype(F32)
            delta = jnp.concatenate([jnp.sum(jnp.where(mask, both, 0.0), -1, keepdims=True), jnp.sum(jnp.where(mask, 0.0, both), -1, keepdims=True)], 0)
            chances = jnp.exp(dot_nt(q, k) * SCALE - two(tops)) * two(factors)
            grads = stacked(grad_pair)
            slope = low(chances * (dot_nt(grads, v) - delta))
            query_part[here, cols] = low(unstacked(dot(slope, k)) * SCALE)
            grad_pairs[c, :, cols] = low(dot_tn(slope, q) * SCALE)
            grad_pairs[c, :, later] = low(dot_tn(low(chances), grads))
        return carry

    lax.fori_loop(0, captions, one, 0)


def self_back(grad, section, lengths, out, wq, wk, wv, projected, low_ref, grad_projected, grad_mixed):
    half = wq.shape[1]
    low_ref[...] = low(grad)
    rows = pl.multiple_of(section * half, half)
    grad_mixed[...] = low(dot_nt(low_ref[...], out[pl.ds(rows, half), :]))
    captions = lengths.shape[0]
    slots = grad.shape[0] // captions
    for c in range(captions):
        keep = keep_mask(lengths[c], slots)
        here = slice(c * slots, (c + 1) * slots)
        for j in range(half // PAIR):
            cols = [slice(i * half + j * PAIR, i * half + (j + 1) * PAIR) for i in range(3)]
            q, k, v = (projected[here, cols[i]] for i in range(3))
            q = stacked(q)
            chances = self_chances(q, k, keep)
            grads = stacked(grad_mixed[here, cols[0]])
            grad_chances = dot_nt(grads, v)
            slope = low(chances * (grad_chances - jnp.sum(grad_chances * chances, -1, keepdims=True)))
            grad_projected[here, cols[0]] = low(unstacked(dot(slope, k)) * SCALE)
            grad_projected[here, cols[1]] = low(dot_tn(slope, q) * SCALE)
            grad_projected[here, cols[2]] = low(dot_tn(low(chances), grads))
    total = jnp.zeros(grad.shape, F32)
    for i, weight in enumerate((wq, wk, wv)):
        total += dot_nt(grad_projected[:, i * half : (i + 1) * half], weight[...])
    return total


def self_back_second_kernel(section, lengths, grad_middle, own, other, first, vecs, query, out, wq, wk, wv, projected, grad_ref, low_ref, grad_queries, grad_projected, part, vec_grad, grad_mixed):
    grad_queries[...] = low(own[...].astype(F32) + other[...].astype(F32))
    inner = dot_nt(grad_queries[...], query[...])
    step, gain_grad, shift_grad = norm_back(first[...], vec(vecs, CROSS_GAIN), inner)
    vec_grad[0:1, :] = gain_grad
    vec_grad[1:2, :] = shift_grad
    grad = step + grad_middle[...]
    grad_ref[...] = grad
    part[...] = low(self_back(grad, section[0], lengths, out, wq, wk, wv, projected, low_ref, grad_projected, grad_mixed))


def feed_back_first_kernel(grad_first, own, other, hidden, vecs, up, down, raised, grad_ref, vec_grad, bias_grad, down_bias_grad, slope, part):
    inner = own[...].astype(F32) + other[...].astype(F32)
    step, gain_grad, shift_grad = norm_back(hidden[...].astype(F32), vec(vecs, LAYER_VECS + SELF_GAIN), inner)
    vec_grad[0:1, :] = gain_grad
    vec_grad[1:2, :] = shift_grad
    grad = low(step + grad_first[...]).astype(F32)
    grad_ref[...] = grad
    feed_back(grad, 0, vecs, up, down, raised, bias_grad, down_bias_grad, slope, part)


def self_back_first_kernel(section, lengths, grad_hidden, own, other, middle, text, vecs, out, wq, wk, wv, projected, grad_ref, low_ref, grad_projected, part, vec_grad, grad_mixed):
    inner = own[...].astype(F32) + other[...].astype(F32)
    step, gain_grad, shift_grad = norm_back(middle[...], vec(vecs, FEED_GAIN), inner)
    vec_grad[0:1, :] = gain_grad
    vec_grad[1:2, :] = shift_grad
    grad = step + grad_hidden[...]
    grad_ref[...] = grad
    total = self_back(grad, section[0], lengths, out, wq, wk, wv, projected, low_ref, grad_projected, grad_mixed)
    part[...] = low(total)
    unit, _ = norm_unit(text[...].astype(F32))
    vec_grad[2:3, :] = jnp.sum(total * unit, 0, keepdims=True)
    vec_grad[3:4, :] = jnp.sum(total, 0, keepdims=True)


def text_grad_kernel(section, grad_middle, own, other, text, vecs, out):
    inner = own[...].astype(F32) + other[...].astype(F32)
    step, _, _ = norm_back(text[...].astype(F32), vec(vecs, SELF_GAIN), inner)
    total = step + grad_middle[...]
    half = out.shape[1]
    out[...] = jnp.where(section[0] == 0, total[:, :half], total[:, half:])


def products_kernel(pieces, *refs):
    out = refs[-1]
    offset = 0
    for left, right, swapped in pieces:
        lhs, rhs = refs[left], refs[right]
        block = 384
        if swapped:
            rows = out.shape[0]
            for i in range(lhs.shape[1] // rows):
                for j in range(rhs.shape[1] // block):
                    out[:, offset : offset + block] = low(dot_tn(lhs[:, i * rows : (i + 1) * rows], rhs[:, j * block : (j + 1) * block]))
                    offset += block
        else:
            for j in range(rhs.shape[1] // block):
                out[:, offset : offset + block] = low(dot_tn(lhs[...], rhs[:, j * block : (j + 1) * block]))
                offset += block


def products(pieces, arrays, name):
    rows = min(arrays[left].shape[1] for left, _, _ in pieces)
    width = sum(arrays[left].shape[1] // rows * arrays[right].shape[1] for left, right, _ in pieces)
    flops = 2 * arrays[0].shape[0] * rows * width
    return call(functools.partial(products_kernel, pieces), [(a, None) for a in arrays], [((rows, width), BF16)], name=name, flops=flops)[0]


def body(
    text,
    image,
    lengths,
    self_gain,
    self_shift,
    heads_in,
    heads_out,
    feed_gain,
    feed_shift,
    up_weight,
    up_bias,
    down_weight,
    down_bias,
    cross_gain,
    cross_shift,
    cross_query,
    cross_keys,
    cross_out,
    cotangent,
):
    section = lax.axis_index("section")
    section_ref = section.astype(jnp.int32).reshape(1)
    count = lax.axis_size("dp")
    captions, half_image, width = image.shape
    rows = text.shape[0]
    piece = heads_in.shape[1]
    cross_piece = cross_query.shape[0]
    half = width // 2
    folds = down_weight.shape[1] // (2 * piece)
    half_ff = folds * width

    def attn_rows(index):
        return heads_in[0].reshape(piece, 3, 2, half)[:, :, index].reshape(piece, 3 * half)

    def feed_rows(index):
        up = up_weight[0].reshape(piece, count, 2, folds, piece)[:, :, index]
        up = up.transpose(0, 2, 1, 3).reshape(piece, half_ff)
        down = down_weight[0].reshape(2, folds, piece, width)[index]
        return jnp.concatenate([up] + [down[i] for i in range(folds)], 1)

    def vec_rows(index):
        bias = up_bias[0].reshape(2, folds, piece)[index]
        return jnp.stack([self_gain[0], self_shift[0], feed_gain[0], feed_shift[0], down_bias[0]] + [bias[i] for i in range(folds)], 1)

    def both_layers(make):
        first, later = make(0), make(1)
        own, got = pick(section, first, later), swap(pick(section, later, first))
        return pick(section, own, got), pick(section, got, own)

    pad = jnp.zeros((piece, 128 - 2 * LAYER_VECS), BF16)
    attn_0, attn_1 = both_layers(lambda i: jnp.concatenate([heads_out[0], attn_rows(i), vec_rows(i)], 1))
    text_all = side(text, swap(text), section, 1)
    feed_0, feed_1 = both_layers(feed_rows)
    cot_all = side(cotangent, swap(cotangent), section, 1)
    core_cols = width + 3 * half
    vec_cols = jnp.concatenate([attn_0[:, core_cols:], attn_1[:, core_cols:], pad], 1)

    cross_own = jnp.concatenate([cross_keys, cross_query, cross_out], 1)
    cross_vec = jnp.stack([cross_gain, cross_shift], 1)
    cross_wide = jnp.concatenate([cross_own, cross_vec, jnp.zeros((cross_piece, 126), BF16)], 1)
    own_cross = ring_gather(cross_wide)
    piece_a = ring_gather(jnp.concatenate([attn_0[:, :core_cols], vec_cols], 1))
    other_cross = swap(own_cross)
    cross_full = side(own_cross, other_cross, section, 0)
    piece_f0 = ring_gather(feed_0)
    piece_d = ring_gather(attn_1[:, :core_cols])
    piece_f1 = ring_gather(feed_1)
    vecs = jnp.concatenate([piece_a[:, core_cols : core_cols + 2 * LAYER_VECS], cross_full[:, 4 * width : 4 * width + 2]], 1).astype(F32).T
    keys_w = cross_full[:, : 2 * width]

    def attn_specs(array):
        return [(array, ((width, half), (0, 2 + i))) for i in range(3)]

    def out_spec(array):
        return (array, ((width, width), (0, 0)))

    def feed_specs(array):
        return [(array, ((width, half_ff), (0, 0))), (array, ((width, half_ff), (0, 1)))]

    query_spec = (cross_full, ((width, width), (0, 2)))
    cross_out_spec = (cross_full, ((width, width), (0, 3)))

    shape_f = ((rows, width), F32)
    shape_b = ((rows, width), BF16)
    shape_half = ((rows, half), BF16)
    shape_qkv = ((rows, 3 * half), BF16)
    shape_raised = ((rows, half_ff), F32)
    shape_active = ((rows, half_ff), BF16)
    lens = (lengths, "s")
    sec = (section_ref, "s")
    whole = lambda a: (a, None)

    pairs = low(dot(image.reshape(captions * half_image, width), keys_w)).reshape(captions, half_image, 2 * width)
    normed_a0, qkv_0, mixed_0 = call(
        self_first_kernel, [lens, whole(text_all), whole(vecs)] + attn_specs(piece_a), [shape_b, shape_qkv, shape_half], name="self_0", flops=2 * rows * width * 3 * half
    )
    other_0 = swap(mixed_0)
    middle_0, normed_f0, raised_0, active_0, part_0 = call(
        feed_first_kernel,
        [sec, whole(text_all), whole(mixed_0), whole(other_0), whole(vecs), out_spec(piece_a)] + feed_specs(piece_f0),
        [shape_f, shape_b, shape_raised, shape_active, shape_b],
        name="feed_0", flops=4 * rows * width * half_ff,
    )
    part_0_other = swap(part_0)
    hidden, normed_a1, qkv_1, mixed_1 = call(
        self_second_kernel,
        [lens, whole(middle_0), whole(part_0), whole(part_0_other), whole(vecs)] + attn_specs(piece_d),
        [shape_b, shape_b, shape_qkv, shape_half],
        name="self_1", flops=2 * rows * width * 3 * half,
    )
    other_1 = swap(mixed_1)
    first_1, normed_c, queries, cross_part, stats = call(
        cross_kernel,
        [sec, whole(hidden), whole(mixed_1), whole(other_1), whole(vecs), out_spec(piece_d), query_spec, whole(pairs)],
        [shape_f, shape_b, shape_b, shape_b, ((rows, 128), F32)],
        name="cross_1", flops=4 * rows * width * width,
    )
    cross_part_other, stats_other = swap(cross_part), swap(stats)
    middle_1, cross_mixed, factor, normed_f1, raised_1, active_1, part_1 = call(
        feed_second_kernel,
        [whole(first_1), whole(cross_part), whole(cross_part_other), whole(stats), whole(stats_other), whole(vecs), cross_out_spec] + feed_specs(piece_f1),
        [shape_f, shape_b, ((rows, 128), F32), shape_b, shape_raised, shape_active, shape_b],
        name="feed_1", flops=4 * rows * width * half_ff,
    )
    own_cols = lambda v: pick(section, v[..., :half], v[..., half:])
    got_part = swap(pick(section, part_1[:, half:], part_1[:, :half]))
    layer_out = own_cols(middle_1) + (own_cols(part_1).astype(F32) + got_part.astype(F32)) + own_cols(vecs[LAYER_VECS + DOWN_BIAS])

    shape_vec = ((8, width), F32)
    shape_bias = ((folds, width), F32)
    shape_one = ((1, width), F32)
    scratch_half = [pltpu.VMEM((rows, half), BF16)]
    bias_grad_1, down_bias_grad_1, slope_1, back_1 = call(
        feed_back_last_kernel, [whole(cot_all), whole(vecs)] + feed_specs(piece_f1) + [whole(raised_1)], [shape_bias, shape_one, shape_active, shape_b], name="feed_back_1", flops=4 * rows * width * half_ff
    )
    back_1_other = swap(back_1)
    feed_grad_1 = products([(0, 1, False), (2, 3, True)], [normed_f1, slope_1, active_1, cot_all], "feed_grads_1")
    feed_got_1 = ring_scatter(feed_grad_1)
    grad_middle_1, grad_low_1, feed_vec_1, query_part, grad_pairs = call(
        cross_back_kernel,
        [whole(cot_all), whole(back_1), whole(back_1_other), whole(middle_1), whole(vecs), cross_out_spec, whole(queries), whole(pairs), whole(stats), whole(factor), whole(cross_mixed)],
        [shape_f, shape_b, shape_vec, shape_b, ((captions, half_image, 2 * width), BF16)],
        scratch=[pltpu.VMEM((rows, width), BF16)],
        name="cross_back", flops=4 * rows * width * width,
    )
    query_part_other = swap(query_part)
    flat_pairs = grad_pairs.reshape(captions * half_image, 2 * width)
    flat_image = image.reshape(captions * half_image, width)
    image_grad = dot_nt(flat_pairs, keys_w).reshape(captions, half_image, width)
    keys_grad = low(dot_tn(flat_image, flat_pairs))
    grad_first_1, head_low_1, grad_queries, grad_qkv_1, self_back_1, cross_vec_1 = call(
        self_back_second_kernel,
        [sec, lens, whole(grad_middle_1), whole(query_part), whole(query_part_other), whole(first_1), whole(vecs), query_spec, out_spec(piece_d)]
        + attn_specs(piece_d) + [whole(qkv_1)],
        [shape_f, shape_b, shape_b, shape_qkv, shape_b, shape_vec],
        scratch=scratch_half, name="self_back_1", flops=4 * rows * width * 3 * half,
    )
    self_back_1_other = swap(self_back_1)
    cross_grad = products([(0, 1, False), (2, 3, False)], [own_cols(normed_c), grad_queries, own_cols(cross_mixed), grad_low_1], "cross_grads")
    cross_vec_cols = jnp.stack([own_cols(cross_vec_1[0]), own_cols(cross_vec_1[1])], 1)
    cross_pack = jnp.concatenate([cross_grad, keys_grad[:half], keys_grad[half:], low(cross_vec_cols), jnp.zeros((half, 126), BF16)], 1)
    cross_got = ring_scatter(cross_pack)
    into_grad_1 = products([(0, 1, False)], [normed_a1, grad_qkv_1], "into_grads_1")
    into_got_1 = ring_scatter(into_grad_1)
    grad_hidden, self_vec_1, bias_grad_0, down_bias_grad_0, slope_0, back_0 = call(
        feed_back_first_kernel,
        [whole(grad_first_1), whole(self_back_1), whole(self_back_1_other), whole(hidden), whole(vecs)] + feed_specs(piece_f0) + [whole(raised_0)],
        [shape_f, shape_vec, shape_bias, shape_one, shape_active, shape_b],
        name="feed_back_0", flops=4 * rows * width * half_ff,
    )
    back_0_other = swap(back_0)
    feed_grad_0 = products([(0, 1, False), (2, 3, True)], [normed_f0, slope_0, active_0, low(grad_hidden)], "feed_grads_0")
    feed_got_0 = ring_scatter(feed_grad_0)
    grad_middle_0, head_low_0, grad_qkv_0, self_back_0, feed_vec_0 = call(
        self_back_first_kernel,
        [sec, lens, whole(grad_hidden), whole(back_0), whole(back_0_other), whole(middle_0), whole(text_all), whole(vecs), out_spec(piece_a)]
        + attn_specs(piece_a) + [whole(qkv_0)],
        [shape_f, shape_b, shape_qkv, shape_b, shape_vec],
        scratch=scratch_half, name="self_back_0", flops=4 * rows * width * 3 * half,
    )
    self_back_0_other = swap(self_back_0)
    mixed_all = pick(section, side(mixed_0, other_0, section, 1), side(mixed_1, other_1, section, 1))
    head_low = pick(section, head_low_0, head_low_1)
    last_grad = products([(0, 1, False), (2, 3, False)], [normed_a0, grad_qkv_0, mixed_all, head_low], "last_grads")
    (text_grad,) = call(
        text_grad_kernel, [sec, whole(grad_middle_0), whole(self_back_0), whole(self_back_0_other), whole(text_all), whole(vecs)], [((rows, half), F32)], name="text_grad"
    )
    vec_rows_out = jnp.concatenate(
        [
            feed_vec_0[2:4],
            jnp.where(section == 0, 0.0, self_vec_1[:2]),
            pick(section, feed_vec_0[:2], feed_vec_1[:2]),
            pick(section, down_bias_grad_0, down_bias_grad_1),
            bias_grad_0,
            bias_grad_1,
        ],
        0,
    )
    vec_grads = jnp.concatenate([low(vec_rows_out).T, jnp.zeros((width, 128 - vec_rows_out.shape[0]), BF16)], 1)
    last_got = ring_scatter(jnp.concatenate([last_grad, vec_grads], 1))
    into_got_0 = last_got[:, : 3 * half]
    out_got = last_got[:, 3 * half : 3 * half + width]
    vec_got = last_got[:, 3 * half + width :]

    def from_both(first, later):
        own, got = pick(section, first, later), swap(low(pick(section, later, first))).astype(F32)
        return pick(section, own, got), pick(section, got, own)

    into_parts = from_both(into_got_0, into_got_1)
    feed_parts = from_both(feed_got_0, feed_got_1)
    zeros_2 = jnp.zeros((piece, 2), F32)
    vec_first = jnp.concatenate([vec_got[:, 0:2], vec_got[:, 7 : 7 + folds]], 1)
    vec_later = jnp.concatenate([vec_got[:, 2:4], vec_got[:, 7 + folds : 7 + 2 * folds]], 1)
    vec_parts = from_both(vec_first, vec_later)
    self_vec = vec_parts[0][:, :2] + vec_parts[1][:, :2]
    heads_in_grad = jnp.stack([v.reshape(piece, 3, half) for v in into_parts], 2).reshape(1, piece, 6 * half)
    up_parts = [v[:, :half_ff].reshape(piece, folds, count, piece).transpose(0, 2, 1, 3) for v in feed_parts]
    up_grad = jnp.stack(up_parts, 2).reshape(1, piece, 2 * half_ff)
    down_parts = [v[:, half_ff:].reshape(piece, folds, width).transpose(1, 0, 2) for v in feed_parts]
    down_grad = jnp.stack(down_parts, 0).reshape(1, 2 * folds * piece, width)
    up_bias_grad = jnp.stack([v[:, 2:].T for v in vec_parts], 0).reshape(1, 2 * folds * piece)
    keys_got = cross_got[:, 2 * width : 6 * width]
    own_keys = pick(section, keys_got[:, : 2 * width], keys_got[:, 2 * width :])
    got_keys = swap(low(pick(section, keys_got[:, 2 * width :], keys_got[:, : 2 * width])))
    return (
        layer_out,
        text_grad,
        image_grad,
        self_vec[:, 0][None],
        self_vec[:, 1][None],
        heads_in_grad,
        out_got[None],
        vec_got[:, 4][None],
        vec_got[:, 5][None],
        up_grad,
        up_bias_grad,
        down_grad,
        vec_got[:, 6][None],
        cross_got[:, 6 * width],
        cross_got[:, 6 * width + 1],
        cross_got[:, :width],
        own_keys + got_keys.astype(F32),
        cross_got[:, width : 2 * width],
    )


def solution(mesh):
    placed = (
        P("dp", "section"),
        P("dp", "section", None),
        P("dp"),
        P("section", "dp"),
        P("section", "dp"),
        P("section", "dp", None),
        P("section", "dp", None),
        P("section", "dp"),
        P("section", "dp"),
        P("section", "dp", None),
        P("section", "dp"),
        P("section", "dp", None),
        P("section", "dp"),
        P(("section", "dp")),
        P(("section", "dp")),
        P(("section", "dp"), None),
        P(("section", "dp"), None),
        P(("section", "dp"), None),
        P("dp", "section"),
    )
    return jax.shard_map(
        body,
        mesh=mesh,
        in_specs=placed,
        out_specs=(P("dp", "section"), P("dp", "section"), P("dp", "section", None)) + placed[3:18],
        check_vma=False,
    )
```

time: 865 us -> 623 us (0.72)
  waiting for transfers between devices: 473 us -> 187 us
  Pallas kernels: 0 us -> 101 us
  starting transfers between devices: 29.6 us -> 121 us
  matrix products: 100 us -> 16.2 us
  local copies, waits for them, and re-layouts: 184 us -> 133 us
  between operations: 17.9 us -> 3.15 us
    reduce_scatter x4 -> x0, waiting for transfers between devices: 264 us -> none  [scatter(): return lax.psum_scatter(value, 'dp', scatter_dimension=0, tiled=True)]
    all_gather x5 -> x0, waiting for transfers between devices: 146 us -> none  [gather(): return lax.all_gather(value, 'dp', axis=0, tiled=True)]
    ppermute x0 -> x90, waiting for transfers between devices: none -> 144 us  [the longest x80 140 us: ring_move(): return lax.ppermute(value, 'dp', ring_steps(shift))]
    ppermute x0 -> x90, starting transfers between devices: none -> 102 us  [the longest x80 100 us: ring_move(): return lax.ppermute(value, 'dp', ring_steps(shift))]
    pallas_call x0 -> x21, Pallas kernels: none -> 101 us  [the longest x16 82.7 us: call(): pl.pallas_call(kernel, grid=(1,), in_specs=specs, out_specs=out_specs, ou...]
    reshape x36 -> x4, local copies, waits for them, and re-layouts: 57.8 us -> 8.09 us  [the longest x1 4.39 us: ring_gather(): return out.reshape(2 * chips * rows, width)]
    dot_general x18 -> x0, matrix products: 31.5 us -> none  [the longest x1 5.54 us: body(): jnp.einsum('chqk,cqhd->ckhd', low(cross_chances), grad_mixed, preferred_e...]
    convert_element_type x4 -> x35, other arithmetic: 1.04 us -> 32.1 us  [low(): return values.astype(BF16)]
  transfers between devices with their start and end apart: 30 -> 110, of which waited for: 23 -> 52; matrix products, arithmetic and copies ran while one was open for 26% -> 23% of each run, Pallas kernels for 0% -> 11%
where the time goes in v2:
time: 623 us; the launch traced here: 611 us
  waiting for transfers between devices  187 us (30%)
  local copies, waits for them, and re-layouts  133 us (21%)
  starting transfers between devices  121 us (19%)
  Pallas kernels  101 us (16%)
  other arithmetic  50.6 us (8%)
  matrix products  16.2 us (3%)
    ppermute x80, waiting for transfers between devices, ring_move(): return lax.ppermute(value, 'dp', ring_steps(shift))  140 us
    ppermute x80, starting transfers between devices, ring_move(): return lax.ppermute(value, 'dp', ring_steps(shift))  100 us
    pallas_call x16, Pallas kernels, call(): pl.pallas_call(kernel, grid=(1,), in_specs=specs, out_specs=out_specs, ou...  82.7 us
    unnamed x316, local copies, waits for them, and re-layouts  55.6 us
    ppermute x20, waiting for transfers between devices, swap(): return lax.ppermute(value, 'section', [(0, 1), (1, 0)])  42.3 us
    convert_element_type x35, other arithmetic, low(): return values.astype(BF16)  32.1 us
    ppermute x20, starting transfers between devices, swap(): return lax.ppermute(value, 'section', [(0, 1), (1, 0)])  19.3 us
    pallas_call x5, Pallas kernels, ring_gather(): pl.pallas_call(functools.partial(gather_kernel, chips), out_shape=jax.Sha...  17.9 us
  transfers between devices with their start and end apart: 110, of which 52 were waited for; matrix products, arithmetic and copies ran while one was open for 23% of the time, Pallas kernels for 11%

profile of v2, /device:TPU:0, one launch (start us, length us, event | category | flops | bytes accessed | tf_op | source)
XLA Modules:
  0.0 611.1 jit_solution(15762202306526887590)
XLA Ops:
  41.6 3.4 collective-permute-done.16.refs_6_
  67.2 5.3 collective-permute-done.3.refs_1_
  74.5 5.7 collective-permute-done.6.refs_5_
  86.2 3.7 collective-permute-done.7.refs_6_
  91.5 4.1 collective-permute-done.39
  96.9 4.1 collective-permute-done.40
  101.0 4.6 collective-permute-done.8
  107.7 3.6 collective-permute-done.9
  120.2 3.2 collective-permute-done.50.refs_6_
  132.6 4.1 collective-permute-done.51
  136.6 3.0 collective-permute-start.30
  140.6 4.3 collective-permute-done.29
  145.0 4.2 assemble.6
  150.6 4.4 copy.260
  160.5 4.9 collective-permute-done.41.refs_8_
  172.8 4.0 assemble.8
  178.5 4.2 assemble.5
  201.3 9.8 %collective-permute-done.20 = bf16[384,3200]{0,1:T(8,128)(2,1)} collective-permute-done((bf16[384,3200]{0,1:T(8,128)(2,1)}, bf16[384,3200]{0,1:T(8,128)(2,1)}, u32[]{:S(2)}, u32[]{:S(2)}) %collective-permute-start.20) | collective-permute-done | bytes 2457632 | tf_op jit(solution)/shard_map/ppermute | solution.py:21
  213.3 3.6 copy-done.3
  223.8 7.3 %copy.264.query.out = bf16[768,3200]{1,0:T(8,128)(2,1)} copy(bf16[768,3200]{0,1:T(8,128)(2,1)} %pad_maximum_fusion) | data formatting | bytes 9830400 | tf_op jit(solution)/shard_map/concatenate | solution.py:29
  233.7 5.4 feed_0.1
  240.8 5.8 convolution_convert_fusion
  246.6 3.0 collective-permute-done.32.other
  253.7 4.0 collective-permute-done.42.other
  257.7 11.0 %cross_1.1 = (f32[256,768]{1,0:T(8,128)S(1)}, bf16[256,768]{1,0:T(8,128)(2,1)S(1)}, bf16[256,768]{1,0:T(8,128)(2,1)S(1)}, bf16[256,768]{1,0:T(8,128)(2,1)S(1)}, f32[256,128]{1,0:T(8,128)S(1)}) custom-call(s32[1]{0:T(128)} %bitcast.section, bf16[256,768]{1,0:T(8,128)(2,1)S(1)} %get-tuple-element.71.hidden, bf16[256,384]{1,0:T(8,128)(2,1)S(1)} %get-tuple-element.72.own, ...), custom_call_target="tpu_custom_call" | custom-call | flops 603979776 | bytes 14336004 | tf_op jit(solution)/shard_map/cross_1/pallas_call | solution.py:209
  275.2 4.8 collective-permute-done.43.other
  280.0 6.9 %feed_1.1 = (f32[256,768]{1,0:T(8,128)S(1)}, bf16[256,768]{1,0:T(8,128)(2,1)S(1)}, f32[256,128]{1,0:T(8,128)S(1)}, bf16[256,768]{1,0:T(8,128)(2,1)S(1)}, f32[256...) custom-call(f32[256,768]{1,0:T(8,128)S(1)} %get-tuple-element.73.first, ...), custom_call_target="tpu_custom_call" | custom-call | flops 1207959552 | bytes 20692992 | tf_op jit(solution)/shard_map/feed_1/pallas_call | solution.py:209
  288.3 4.2 feed_back_1.1
  294.6 4.0 feed_grads_1.1
  298.6 3.2 dynamic-slice_bitcast_fusion
  304.3 13.3 %cross_back.1 = (f32[256,768]{1,0:T(8,128)S(1)}, bf16[256,768]{1,0:T(8,128)(2,1)S(1)}, f32[8,768]{1,0:T(8,128)S(1)}, bf16[256,768]{1,0:T(8,128)(2,1)S(1)}, bf16[4,288,1536]{2,1,0:T(8,128)(2,1)}) custom-call(bf16[256,768]{1,0:T(8,128)(2,1)S(1)} %pad_maximum_fusion.5.cot.refs_3_, bf16[256,768]{1,0:T(8,128)(2,1)S(1)} %get-tuple-element.79.own, ...), custom_call_target="tpu_custom_call" | custom-call | flops 603979776 | bytes 16654336 | tf_op jit(solution)/shard_map/cross_back/pallas_call | solution.py:209
  317.6 6.9 %fusion.2 = f32[4,288,768]{2,1,0:T(8,128)} fusion(bf16[4,288,1536]{2,1,0:T(8,128)(2,1)} %get-tuple-element.94, bf16[384,3200]{0,1:T(8,128)(2,1)S(1)} %copy-done.121, bf16[384,3200]{0,1:T(8,128)(2,1)S(1)} %copy-done.119), kind=kOutput, calls=%fused_computation.11 | convolution fusion | flops 2722627584 | bytes 11993088 | tf_op jit(solution)/shard_map/dot_general | solution.py:156
  324.5 3.5 fusion
  331.2 7.6 %collective-permute-done.57.other = bf16[256,768]{1,0:T(8,128)(2,1)S(1)} collective-permute-done((bf16[256,768]{1,0:T(8,128)(2,1)S(1)}, bf16[256,768]{1,0:T(8,128)(2,1)S(1)}, u32[]{:S(2)}, u32[]{:S(2)}) %collective-permute-start.57) | collective-permute-done | bytes 393248 | tf_op jit(solution)/shard_map/ppermute | solution.py:21
  338.8 10.2 %self_back_1.1 = (f32[256,768]{1,0:T(8,128)S(1)}, bf16[256,768]{1,0:T(8,128)(2,1)S(1)}, bf16[256,768]{1,0:T(8,128)(2,1)S(1)}, bf16[256,1152]{1,0:T(8,128)(2,1)S(...) custom-call(s32[1]{0:T(128)} %bitcast.section, s32[4]{0:T(128)S(1)} %copy-done.116, ...), custom_call_target="tpu_custom_call" | custom-call | flops 905969664 | bytes 22290452 | tf_op jit(solution)/shard_map/self_back_1/pallas_call | solution.py:209
  362.9 6.6 %concatenate.155 = bf16[384,4736]{1,0:T(8,128)(2,1)} concatenate(bf16[384,1536]{1,0:T(8,128)(2,1)S(1)} %cross_grads.1, bf16[384,1536]{1,0:T(8,128)(2,1)} %get-tuple-element.173, bf16[384,1536]{1,0:T(8,128)(2,1)} %get-tuple-element.172, bf16[384,1]{1,0:T(8,128)(2,1)} %copy.278, bf16[384,1]{1,0:T(8,128)(2,1)S(1)} %copy.279, bf16[384,126]{1,0:T(8,128)(2,1)} %broadcast_in_dim.25), dimensions={1} | concatenate | bytes 7274496 | tf_op jit(solution)/shard_map/concatenate | solution.py:655
  369.5 3.0 dynamic-slice_bitcast_fusion.2
  373.1 5.1 feed_back_0.1
  378.7 4.0 feed_grads_0.1
  383.8 3.4 dynamic-slice_bitcast_fusion.1
  390.0 9.0 %self_back_0.1 = (f32[256,768]{1,0:T(8,128)S(1)}, bf16[256,768]{1,0:T(8,128)(2,1)S(1)}, bf16[256,1152]{1,0:T(8,128)(2,1)S(1)}, bf16[256,768]{1,0:T(8,128)(2,1)S(1)}, f32[8,768]{1,0:T(8,128)S(1)}) custom-call(s32[1]{0:T(128)} %bitcast.section, s32[4]{0:T(128)S(1)} %copy-done.116, f32[256,768]{1,0:T(8,128)S(1)} %get-tuple-element.89.grad_hidden, ...), custom_call_target="tpu_custom_call" | custom-call | flops 905969664 | bytes 18161684 | tf_op jit(solution)/shard_map/self_back_0/pallas_call | solution.py:209
  417.7 5.1 concatenate.136
  440.5 3.7 collective-permute-done.101
  445.8 5.7 collective-permute-done.92
  453.4 5.4 collective-permute-done.102
  461.9 3.6 collective-permute-done.93
  483.6 3.7 collective-permute-done.106
  488.9 4.1 collective-permute-done.63
  496.3 3.9 collective-permute-done.107
  503.4 3.7 collective-permute-start.104
  507.1 3.3 collective-permute-start.97
  510.6 6.2 %collective-permute-done.97 = bf16[48,3072]{1,0:T(8,128)(2,1)S(1)} collective-permute-done((bf16[48,3072]{1,0:T(8,128)(2,1)S(1)}, bf16[48,3072]{1,0:T(8,128)(2,1)S(1)}, u32[]{:S(2)}, u32[]{:S(2)}) %collective-permute-start.97) | collective-permute-done | bytes 294944 | tf_op jit(solution)/shard_map/ppermute | solution.py:48
  524.4 3.7 collective-permute-done.67
  530.3 3.8 collective-permute-done.108
  536.7 3.5 collective-permute-done.109
  542.0 6.0 collective-permute-done.68
  548.1 3.5 collective-permute-start.83
  551.6 4.2 collective-permute-done.83
  560.0 3.5 collective-permute-done.69
  575.8 3.3 collective-permute-done.87
  582.6 4.6 collective-permute-done.88
  591.7 3.9 collective-permute-done.89
  599.1 4.9 collective-permute-done.99
  607.4 3.2 reshape.487
  (658 shorter events, 295.4 us)
Async XLA Ops:
  3.3 24.7 %collective-permute-start.14 = (bf16[24,3200]{1,0:T(8,128)(2,1)S(1)}, bf16[24,3200]{1,0:T(8,128)(2,1)S(1)}, u32[]{:S(2)}, u32[]{:S(2)}) collective-permute-start(bf16[24,3200]{1,0:T(8,128)(2,1)S(1)} %concatenate.123.refs_3_), channel_id=1, source_target_pairs={{0,2},{1,3},{4,0},{5,1},{8,4},{9,5},{12,8},{13,9},{14,12},{15,13},... | collective-permute-start | bytes 460808 | tf_op jit(solution)/shard_map/ppermute | solution.py:48
  6.3 23.7 %collective-permute-start.11 = (bf16[24,3200]{1,0:T(8,128)(2,1)S(1)}, bf16[24,3200]{1,0:T(8,128)(2,1)S(1)}, u32[]{:S(2)}, u32[]{:S(2)}) collective-permute-start(bf16[24,3200]{1,0:T(8,128)(2,1)S(1)} %concatenate.123.refs_3_), channel_id=1, source_target_pairs={{0,4},{1,5},{4,8},{5,9},{8,12},{9,13},{12,14},{13,15},{14,10},{15,... | collective-permute-start | bytes 460808 | tf_op jit(solution)/shard_map/ppermute | solution.py:48
  15.6 14.5 %collective-permute-start.1 = (bf16[48,1927]{1,0:T(8,128)(2,1)}, bf16[48,1927]{1,0:T(8,128)(2,1)}, u32[]{:S(2)}, u32[]{:S(2)}) collective-permute-start(bf16[48,1927]{1,0:T(8,128)(2,1)} %broadcast_select_fusion.10), channel_id=1, source_target_pairs={{0,16},{16,0},{1,17},{17,1},{2,18},{18,2},{3,19},{19,3},{4,20},{20... | collective-permute-start | bytes 554984 | tf_op jit(solution)/shard_map/ppermute | solution.py:21
  27.8 8.2 %collective-permute-start.22 = (bf16[48,3072]{1,0:T(8,128)(2,1)}, bf16[48,3072]{1,0:T(8,128)(2,1)}, u32[]{:S(2)}, u32[]{:S(2)}) collective-permute-start(bf16[48,3072]{1,0:T(8,128)(2,1)} %broadcast_select_fusion.6), channel_id=1, source_target_pairs={{0,16},{16,0},{1,17},{17,1},{2,18},{18,2},{3,19},{19,3},{4,20},{20... | collective-permute-start | bytes 884744 | tf_op jit(solution)/shard_map/ppermute | solution.py:21
  28.0 9.5 %collective-permute-start.15 = (bf16[24,3200]{1,0:T(8,128)(2,1)S(1)}, bf16[24,3200]{1,0:T(8,128)(2,1)}, u32[]{:S(2)}, u32[]{:S(2)}) collective-permute-start(bf16[24,3200]{1,0:T(8,128)(2,1)S(1)} %collective-permute-done.14.refs_4_), channel_id=1, source_target_pairs={{0,2},{1,3},{4,0},{5,1},{8,4},{9,5},{12,8},{13,9},{14,12},{15,13},... | collective-permute-start | bytes 460808 | tf_op jit(solution)/shard_map/ppermute | solution.py:48
  30.0 9.1 %collective-permute-start.12 = (bf16[24,3200]{1,0:T(8,128)(2,1)S(1)}, bf16[24,3200]{1,0:T(8,128)(2,1)}, u32[]{:S(2)}, u32[]{:S(2)}) collective-permute-start(bf16[24,3200]{1,0:T(8,128)(2,1)S(1)} %collective-permute-done.11.refs_2_), channel_id=1, source_target_pairs={{0,4},{1,5},{4,8},{5,9},{8,12},{9,13},{12,14},{13,15},{14,10},{15,... | collective-permute-start | bytes 460808 | tf_op jit(solution)/shard_map/ppermute | solution.py:48
  31.8 17.3 %collective-permute-start.36 = (bf16[48,1920]{1,0:T(8,128)(2,1)S(1)}, bf16[48,1920]{1,0:T(8,128)(2,1)S(1)}, u32[]{:S(2)}, u32[]{:S(2)}) collective-permute-start(bf16[48,1920]{1,0:T(8,128)(2,1)S(1)} %slice.460.refs_3_), channel_id=1, source_target_pairs={{0,2},{1,3},{4,0},{5,1},{8,4},{9,5},{12,8},{13,9},{14,12},{15,13},... | collective-permute-start | bytes 552968 | tf_op jit(solution)/shard_map/ppermute | solution.py:48
  36.0 29.5 %collective-permute-start.5 = (bf16[48,2048]{1,0:T(8,128)(2,1)S(1)}, bf16[48,2048]{1,0:T(8,128)(2,1)S(1)}, u32[]{:S(2)}, u32[]{:S(2)}) collective-permute-start(bf16[48,2048]{1,0:T(8,128)(2,1)S(1)} %concatenate.121.refs_3_), channel_id=1, source_target_pairs={{0,2},{1,3},{4,0},{5,1},{8,4},{9,5},{12,8},{13,9},{14,12},{15,13},... | collective-permute-start | bytes 589832 | tf_op jit(solution)/shard_map/ppermute | solution.py:48
  41.0 13.3 %collective-permute-start.34 = (bf16[48,1920]{1,0:T(8,128)(2,1)S(1)}, bf16[48,1920]{1,0:T(8,128)(2,1)S(1)}, u32[]{:S(2)}, u32[]{:S(2)}) collective-permute-start(bf16[48,1920]{1,0:T(8,128)(2,1)S(1)} %collective-permute-done.33.refs_2_), channel_id=1, source_target_pairs={{0,4},{1,5},{4,8},{5,9},{8,12},{9,13},{12,14},{13,15},{14,10},{15,... | collective-permute-start | bytes 552968 | tf_op jit(solution)/shard_map/ppermute | solution.py:48
  51.1 30.7 %collective-permute-start.48 = (bf16[48,3072]{1,0:T(8,128)(2,1)S(1)}, bf16[48,3072]{1,0:T(8,128)(2,1)S(1)}, u32[]{:S(2)}, u32[]{:S(2)}) collective-permute-start(bf16[48,3072]{1,0:T(8,128)(2,1)S(1)} %get-tuple-element.176.refs_3_), channel_id=1, source_target_pairs={{0,2},{1,3},{4,0},{5,1},{8,4},{9,5},{12,8},{13,9},{14,12},{15,13},... | collective-permute-start | bytes 884744 | tf_op jit(solution)/shard_map/ppermute | solution.py:48
  52.7 8.7 %collective-permute-start.37 = (bf16[48,1920]{1,0:T(8,128)(2,1)S(1)}, bf16[48,1920]{1,0:T(8,128)(2,1)S(1)}, u32[]{:S(2)}, u32[]{:S(2)}) collective-permute-start(bf16[48,1920]{1,0:T(8,128)(2,1)S(1)} %collective-permute-done.36.refs_4_), channel_id=1, source_target_pairs={{0,2},{1,3},{4,0},{5,1},{8,4},{9,5},{12,8},{13,9},{14,12},{15,13},... | collective-permute-start | bytes 552968 | tf_op jit(solution)/shard_map/ppermute | solution.py:48
  54.3 8.7 %collective-permute-start.35 = (bf16[48,1920]{1,0:T(8,128)(2,1)S(1)}, bf16[48,1920]{1,0:T(8,128)(2,1)S(1)}, u32[]{:S(2)}, u32[]{:S(2)}) collective-permute-start(bf16[48,1920]{1,0:T(8,128)(2,1)S(1)} %collective-permute-done.34.refs_1_), channel_id=1, source_target_pairs={{0,4},{1,5},{4,8},{5,9},{8,12},{9,13},{12,14},{13,15},{14,10},{15,... | collective-permute-start | bytes 552968 | tf_op jit(solution)/shard_map/ppermute | solution.py:48
  57.0 26.5 %collective-permute-start.45 = (bf16[48,3072]{1,0:T(8,128)(2,1)S(1)}, bf16[48,3072]{1,0:T(8,128)(2,1)S(1)}, u32[]{:S(2)}, u32[]{:S(2)}) collective-permute-start(bf16[48,3072]{1,0:T(8,128)(2,1)S(1)} %get-tuple-element.176.refs_3_), channel_id=1, source_target_pairs={{0,4},{1,5},{4,8},{5,9},{8,12},{9,13},{12,14},{13,15},{14,10},{15,... | collective-permute-start | bytes 884744 | tf_op jit(solution)/shard_map/ppermute | solution.py:48
  61.4 11.0 %collective-permute-start.3 = (bf16[48,2048]{1,0:T(8,128)(2,1)S(1)}, bf16[48,2048]{1,0:T(8,128)(2,1)S(1)}, u32[]{:S(2)}, u32[]{:S(2)}) collective-permute-start(bf16[48,2048]{1,0:T(8,128)(2,1)S(1)} %collective-permute-done.2.refs_2_), channel_id=1, source_target_pairs={{0,4},{1,5},{4,8},{5,9},{8,12},{9,13},{12,14},{13,15},{14,10},{15,... | collective-permute-start | bytes 589832 | tf_op jit(solution)/shard_map/ppermute | solution.py:48
  63.0 11.0 %collective-permute-start.38 = (bf16[48,1920]{1,0:T(8,128)(2,1)S(1)}, bf16[48,1920]{1,0:T(8,128)(2,1)S(1)}, u32[]{:S(2)}, u32[]{:S(2)}) collective-permute-start(bf16[48,1920]{1,0:T(8,128)(2,1)S(1)} %collective-permute-done.37.refs_5_), channel_id=1, source_target_pairs={{0,2},{1,3},{4,0},{5,1},{8,4},{9,5},{12,8},{13,9},{14,12},{15,13},... | collective-permute-start | bytes 552968 | tf_op jit(solution)/shard_map/ppermute | solution.py:48
  65.5 18.8 %collective-permute-start.23 = (bf16[48,3072]{1,0:T(8,128)(2,1)S(1)}, bf16[48,3072]{1,0:T(8,128)(2,1)S(1)}, u32[]{:S(2)}, u32[]{:S(2)}) collective-permute-start(bf16[48,3072]{1,0:T(8,128)(2,1)S(1)} %get-tuple-element.177.refs_3_), channel_id=1, source_target_pairs={{0,4},{1,5},{4,8},{5,9},{8,12},{9,13},{12,14},{13,15},{14,10},{15,... | collective-permute-start | bytes 884744 | tf_op jit(solution)/shard_map/ppermute | solution.py:48
  74.0 11.5 %collective-permute-start.4 = (bf16[48,2048]{1,0:T(8,128)(2,1)S(1)}, bf16[48,2048]{1,0:T(8,128)(2,1)S(1)}, u32[]{:S(2)}, u32[]{:S(2)}) collective-permute-start(bf16[48,2048]{1,0:T(8,128)(2,1)S(1)} %collective-permute-done.3.refs_1_), channel_id=1, source_target_pairs={{0,4},{1,5},{4,8},{5,9},{8,12},{9,13},{12,14},{13,15},{14,10},{15,... | collective-permute-start | bytes 589832 | tf_op jit(solution)/shard_map/ppermute | solution.py:48
  80.3 32.4 %collective-permute-start.26 = (bf16[48,3072]{1,0:T(8,128)(2,1)S(1)}, bf16[48,3072]{1,0:T(8,128)(2,1)S(1)}, u32[]{:S(2)}, u32[]{:S(2)}) collective-permute-start(bf16[48,3072]{1,0:T(8,128)(2,1)S(1)} %get-tuple-element.177.refs_3_), channel_id=1, source_target_pairs={{0,2},{1,3},{4,0},{5,1},{8,4},{9,5},{12,8},{13,9},{14,12},{15,13},... | collective-permute-start | bytes 884744 | tf_op jit(solution)/shard_map/ppermute | solution.py:48
  83.5 29.9 %collective-permute-start.49 = (bf16[48,3072]{1,0:T(8,128)(2,1)S(1)}, bf16[48,3072]{1,0:T(8,128)(2,1)S(1)}, u32[]{:S(2)}, u32[]{:S(2)}) collective-permute-start(bf16[48,3072]{1,0:T(8,128)(2,1)S(1)} %collective-permute-done.48.refs_4_), channel_id=1, source_target_pairs={{0,2},{1,3},{4,0},{5,1},{8,4},{9,5},{12,8},{13,9},{14,12},{15,13},... | collective-permute-start | bytes 884744 | tf_op jit(solution)/shard_map/ppermute | solution.py:48
  84.3 30.8 %collective-permute-start.46 = (bf16[48,3072]{1,0:T(8,128)(2,1)S(1)}, bf16[48,3072]{1,0:T(8,128)(2,1)S(1)}, u32[]{:S(2)}, u32[]{:S(2)}) collective-permute-start(bf16[48,3072]{1,0:T(8,128)(2,1)S(1)} %collective-permute-done.45.refs_2_), channel_id=1, source_target_pairs={{0,4},{1,5},{4,8},{5,9},{8,12},{9,13},{12,14},{13,15},{14,10},{15,... | collective-permute-start | bytes 884744 | tf_op jit(solution)/shard_map/ppermute | solution.py:48
  85.5 21.7 %collective-permute-start.24 = (bf16[48,3072]{1,0:T(8,128)(2,1)S(1)}, bf16[48,3072]{1,0:T(8,128)(2,1)S(1)}, u32[]{:S(2)}, u32[]{:S(2)}) collective-permute-start(bf16[48,3072]{1,0:T(8,128)(2,1)S(1)} %collective-permute-done.23.refs_2_), channel_id=1, source_target_pairs={{0,4},{1,5},{4,8},{5,9},{8,12},{9,13},{12,14},{13,15},{14,10},{15,... | collective-permute-start | bytes 884744 | tf_op jit(solution)/shard_map/ppermute | solution.py:48
  107.2 8.9 %collective-permute-start.25 = (bf16[48,3072]{1,0:T(8,128)(2,1)S(1)}, bf16[48,3072]{1,0:T(8,128)(2,1)S(1)}, u32[]{:S(2)}, u32[]{:S(2)}) collective-permute-start(bf16[48,3072]{1,0:T(8,128)(2,1)S(1)} %collective-permute-done.24.refs_1_), channel_id=1, source_target_pairs={{0,4},{1,5},{4,8},{5,9},{8,12},{9,13},{12,14},{13,15},{14,10},{15,... | collective-permute-start | bytes 884744 | tf_op jit(solution)/shard_map/ppermute | solution.py:48
  111.3 45.8 %collective-permute-start = (bf16[256,384]{1,0:T(8,128)(2,1)}, bf16[256,384]{1,0:T(8,128)(2,1)}, u32[]{:S(2)}, u32[]{:S(2)}) collective-permute-start(bf16[256,384]{1,0:T(8,128)(2,1)} %param.19), channel_id=1, source_target_pairs={{0,16},{16,0},{1,17},{17,1},{2,18},{18,2},{3,19},{19,3},{4,20},{20... | collective-permute-start | bytes 589832 | tf_op jit(solution)/shard_map/ppermute | solution.py:21
  112.7 45.4 %collective-permute-start.55 = (bf16[256,384]{1,0:T(8,128)(2,1)}, bf16[256,384]{1,0:T(8,128)(2,1)}, u32[]{:S(2)}, u32[]{:S(2)}) collective-permute-start(bf16[256,384]{1,0:T(8,128)(2,1)} %param.37), channel_id=1, source_target_pairs={{0,16},{16,0},{1,17},{17,1},{2,18},{18,2},{3,19},{19,3},{4,20},{20... | collective-permute-start | bytes 589832 | tf_op jit(solution)/shard_map/ppermute | solution.py:21
  115.1 8.3 %collective-permute-start.50 = (bf16[48,3072]{1,0:T(8,128)(2,1)S(1)}, bf16[48,3072]{1,0:T(8,128)(2,1)S(1)}, u32[]{:S(2)}, u32[]{:S(2)}) collective-permute-start(bf16[48,3072]{1,0:T(8,128)(2,1)S(1)} %collective-permute-done.49.refs_5_), channel_id=1, source_target_pairs={{0,2},{1,3},{4,0},{5,1},{8,4},{9,5},{12,8},{13,9},{14,12},{15,13},... | collective-permute-start | bytes 884744 | tf_op jit(solution)/shard_map/ppermute | solution.py:48
  116.2 8.9 %collective-permute-start.47 = (bf16[48,3072]{1,0:T(8,128)(2,1)S(1)}, bf16[48,3072]{1,0:T(8,128)(2,1)S(1)}, u32[]{:S(2)}, u32[]{:S(2)}) collective-permute-start(bf16[48,3072]{1,0:T(8,128)(2,1)S(1)} %collective-permute-done.46.refs_1_), channel_id=1, source_target_pairs={{0,4},{1,5},{4,8},{5,9},{8,12},{9,13},{12,14},{13,15},{14,10},{15,... | collective-permute-start | bytes 884744 | tf_op jit(solution)/shard_map/ppermute | solution.py:48
  120.2 24.7 %collective-permute-start.19 = (bf16[8,24,3200]{2,1,0:T(8,128)(2,1)S(1)}, bf16[8,24,3200]{2,1,0:T(8,128)(2,1)S(1)}, u32[]{:S(2)}, u32[]{:S(2)}) collective-permute-start(bf16[8,24,3200]{2,1,0:T(8,128)(2,1)S(1)} %get-tuple-element.148), channel_id=1, source_target_pairs={{0,1},{1,0},{2,3},{3,2},{4,5},{5,4},{6,7},{7,6},{8,9},{9,8},{10,11... | collective-permute-start | bytes 3686408 | tf_op jit(solution)/shard_map/ppermute | solution.py:52
  123.4 8.0 %collective-permute-start.28 = (bf16[48,3072]{1,0:T(8,128)(2,1)S(1)}, bf16[48,3072]{1,0:T(8,128)(2,1)S(1)}, u32[]{:S(2)}, u32[]{:S(2)}) collective-permute-start(bf16[48,3072]{1,0:T(8,128)(2,1)S(1)} %collective-permute-done.27.refs_5_), channel_id=1, source_target_pairs={{0,2},{1,3},{4,0},{5,1},{8,4},{9,5},{12,8},{13,9},{14,12},{15,13},... | collective-permute-start | bytes 884744 | tf_op jit(solution)/shard_map/ppermute | solution.py:48
  125.0 14.7 %collective-permute-start.52 = (bf16[24,3072]{1,0:T(8,128)(2,1)S(1)}, bf16[24,3072]{1,0:T(8,128)(2,1)S(1)}, u32[]{:S(2)}, u32[]{:S(2)}) collective-permute-start(bf16[24,3072]{1,0:T(8,128)(2,1)S(1)} %slice.466), channel_id=1, source_target_pairs={{0,2},{1,3},{4,0},{5,1},{8,4},{9,5},{12,8},{13,9},{14,12},{15,13},... | collective-permute-start | bytes 442376 | tf_op jit(solution)/shard_map/ppermute | solution.py:48
  136.6 8.3 %collective-permute-start.30 = (bf16[24,3072]{1,0:T(8,128)(2,1)S(1)}, bf16[24,3072]{1,0:T(8,128)(2,1)S(1)}, u32[]{:S(2)}, u32[]{:S(2)}) collective-permute-start(bf16[24,3072]{1,0:T(8,128)(2,1)S(1)} %slice.459), channel_id=1, source_target_pairs={{0,2},{1,3},{4,0},{5,1},{8,4},{9,5},{12,8},{13,9},{14,12},{15,13},... | collective-permute-start | bytes 442376 | tf_op jit(solution)/shard_map/ppermute | solution.py:48
  144.9 39.6 %collective-permute-start.53 = (bf16[8,48,3072]{2,1,0:T(8,128)(2,1)}, bf16[8,48,3072]{2,1,0:T(8,128)(2,1)}, u32[]{:S(2)}, u32[]{:S(2)}) collective-permute-start(bf16[8,48,3072]{2,1,0:T(8,128)(2,1)} %bitcast_dynamic-update-slice_fusion), channel_id=1, source_target_pairs={{0,1},{1,0},{2,3},{3,2},{4,5},{5,4},{6,7},{7,6},{8,9},{9,8},{10,11... | collective-permute-start | bytes 7077896 | tf_op jit(solution)/shard_map/ppermute | solution.py:52
  155.0 56.1 %collective-permute-start.20 = (bf16[384,3200]{0,1:T(8,128)(2,1)}, bf16[384,3200]{0,1:T(8,128)(2,1)}, u32[]{:S(2)}, u32[]{:S(2)}) collective-permute-start(bf16[384,3200]{0,1:T(8,128)(2,1)} %copy.260), channel_id=1, source_target_pairs={{0,16},{16,0},{1,17},{17,1},{2,18},{18,2},{3,19},{19,3},{4,20},{20... | collective-permute-start | bytes 7372808 | tf_op jit(solution)/shard_map/ppermute | solution.py:21
  156.2 40.1 %collective-permute-start.31 = (bf16[8,48,3072]{2,1,0:T(8,128)(2,1)}, bf16[8,48,3072]{2,1,0:T(8,128)(2,1)}, u32[]{:S(2)}, u32[]{:S(2)}) collective-permute-start(bf16[8,48,3072]{2,1,0:T(8,128)(2,1)} %bitcast_dynamic-update-slice_fusion.8), channel_id=1, source_target_pairs={{0,1},{1,0},{2,3},{3,2},{4,5},{5,4},{6,7},{7,6},{8,9},{9,8},{10,11... | collective-permute-start | bytes 7077896 | tf_op jit(solution)/shard_map/ppermute | solution.py:52
  157.1 21.3 %collective-permute-start.10 = (bf16[8,48,2048]{2,1,0:T(8,128)(2,1)}, bf16[8,48,2048]{2,1,0:T(8,128)(2,1)}, u32[]{:S(2)}, u32[]{:S(2)}) collective-permute-start(bf16[8,48,2048]{2,1,0:T(8,128)(2,1)} %bitcast_dynamic-update-slice_fusion.16), channel_id=1, source_target_pairs={{0,1},{1,0},{2,3},{3,2},{4,5},{5,4},{6,7},{7,6},{8,9},{9,8},{10,11... | collective-permute-start | bytes 4718600 | tf_op jit(solution)/shard_map/ppermute | solution.py:52
  220.7 10.5 %collective-permute-start.21 = (bf16[256,384]{1,0:T(8,128)(2,1)S(1)}, bf16[256,384]{1,0:T(8,128)(2,1)S(1)}, u32[]{:S(2)}, u32[]{:S(2)}) collective-permute-start(bf16[256,384]{1,0:T(8,128)(2,1)S(1)} %get-tuple-element.68.own), channel_id=1, source_target_pairs={{0,16},{16,0},{1,17},{17,1},{2,18},{18,2},{3,19},{19,3},{4,20},{20... | collective-permute-start | bytes 589832 | tf_op jit(solution)/shard_map/ppermute | solution.py:21
  239.1 10.5 %collective-permute-start.32 = (bf16[256,768]{1,0:T(8,128)(2,1)S(1)}, bf16[256,768]{1,0:T(8,128)(2,1)S(1)}, u32[]{:S(2)}, u32[]{:S(2)}) collective-permute-start(bf16[256,768]{1,0:T(8,128)(2,1)S(1)} %get-tuple-element.70.own), channel_id=1, source_target_pairs={{0,16},{16,0},{1,17},{17,1},{2,18},{18,2},{3,19},{19,3},{4,20},{20... | collective-permute-start | bytes 1179656 | tf_op jit(solution)/shard_map/ppermute | solution.py:21
  270.4 9.6 %collective-permute-start.43 = (bf16[256,768]{1,0:T(8,128)(2,1)S(1)}, bf16[256,768]{1,0:T(8,128)(2,1)S(1)}, u32[]{:S(2)}, u32[]{:S(2)}) collective-permute-start(bf16[256,768]{1,0:T(8,128)(2,1)S(1)} %get-tuple-element.74.own), channel_id=1, source_target_pairs={{0,16},{16,0},{1,17},{17,1},{2,18},{18,2},{3,19},{19,3},{4,20},{20... | collective-permute-start | bytes 1179656 | tf_op jit(solution)/shard_map/ppermute | solution.py:21
  292.5 10.0 %collective-permute-start.54 = (bf16[256,384]{1,0:T(8,128)(2,1)S(1)}, bf16[256,384]{1,0:T(8,128)(2,1)S(1)}, u32[]{:S(2)}, u32[]{:S(2)}) collective-permute-start(bf16[256,384]{1,0:T(8,128)(2,1)S(1)} %broadcast_select_fusion.18), channel_id=1, source_target_pairs={{0,16},{16,0},{1,17},{17,1},{2,18},{18,2},{3,19},{19,3},{4,20},{20... | collective-permute-start | bytes 589832 | tf_op jit(solution)/shard_map/ppermute | solution.py:21
  294.2 10.1 %collective-permute-start.56 = (bf16[256,768]{1,0:T(8,128)(2,1)S(1)}, bf16[256,768]{1,0:T(8,128)(2,1)S(1)}, u32[]{:S(2)}, u32[]{:S(2)}) collective-permute-start(bf16[256,768]{1,0:T(8,128)(2,1)S(1)} %get-tuple-element.79.own), channel_id=1, source_target_pairs={{0,16},{16,0},{1,17},{17,1},{2,18},{18,2},{3,19},{19,3},{4,20},{20... | collective-permute-start | bytes 1179656 | tf_op jit(solution)/shard_map/ppermute | solution.py:21
  301.8 130.2 %collective-permute-start.90 = (bf16[8,48,3072]{2,1,0:T(8,128)(2,1)}, bf16[8,48,3072]{2,1,0:T(8,128)(2,1)}, u32[]{:S(2)}, u32[]{:S(2)}) collective-permute-start(bf16[8,48,3072]{2,1,0:T(8,128)(2,1)} %dynamic-slice_bitcast_fusion), channel_id=1, source_target_pairs={{0,1},{1,0},{2,3},{3,2},{4,5},{5,4},{6,7},{7,6},{8,9},{9,8},{10,11... | collective-permute-start | bytes 7077896 | tf_op jit(solution)/shard_map/ppermute | solution.py:52
  328.0 10.8 %collective-permute-start.57 = (bf16[256,768]{1,0:T(8,128)(2,1)S(1)}, bf16[256,768]{1,0:T(8,128)(2,1)S(1)}, u32[]{:S(2)}, u32[]{:S(2)}) collective-permute-start(bf16[256,768]{1,0:T(8,128)(2,1)S(1)} %get-tuple-element.84.own), channel_id=1, source_target_pairs={{0,16},{16,0},{1,17},{17,1},{2,18},{18,2},{3,19},{19,3},{4,20},{20... | collective-permute-start | bytes 1179656 | tf_op jit(solution)/shard_map/ppermute | solution.py:21
  353.2 19.8 %collective-permute-start.58 = (bf16[256,768]{1,0:T(8,128)(2,1)}, bf16[256,768]{1,0:T(8,128)(2,1)}, u32[]{:S(2)}, u32[]{:S(2)}) collective-permute-start(bf16[256,768]{1,0:T(8,128)(2,1)} %get-tuple-element.87.own), channel_id=1, source_target_pairs={{0,16},{16,0},{1,17},{17,1},{2,18},{18,2},{3,19},{19,3},{4,20},{20... | collective-permute-start | bytes 1179656 | tf_op jit(solution)/shard_map/ppermute | solution.py:21
  358.8 24.0 %collective-permute-start.71 = (bf16[8,48,1152]{2,1,0:T(8,128)(2,1)}, bf16[8,48,1152]{2,1,0:T(8,128)(2,1)}, u32[]{:S(2)}, u32[]{:S(2)}) collective-permute-start(bf16[8,48,1152]{2,1,0:T(8,128)(2,1)} %dynamic-slice_bitcast_fusion.4), channel_id=1, source_target_pairs={{0,1},{1,0},{2,3},{3,2},{4,5},{5,4},{6,7},{7,6},{8,9},{9,8},{10,11... | collective-permute-start | bytes 2654216 | tf_op jit(solution)/shard_map/ppermute | solution.py:52
  372.5 60.8 %collective-permute-start.100 = (bf16[8,24,4736]{2,1,0:T(8,128)(2,1)}, bf16[8,24,4736]{2,1,0:T(8,128)(2,1)}, u32[]{:S(2)}, u32[]{:S(2)}) collective-permute-start(bf16[8,24,4736]{2,1,0:T(8,128)(2,1)} %dynamic-slice_bitcast_fusion.2), channel_id=1, source_target_pairs={{0,1},{1,0},{2,3},{3,2},{4,5},{5,4},{6,7},{7,6},{8,9},{9,8},{10,11... | collective-permute-start | bytes 5455880 | tf_op jit(solution)/shard_map/ppermute | solution.py:52
  378.2 11.7 %collective-permute-start.59 = (bf16[256,768]{1,0:T(8,128)(2,1)S(1)}, bf16[256,768]{1,0:T(8,128)(2,1)S(1)}, u32[]{:S(2)}, u32[]{:S(2)}) collective-permute-start(bf16[256,768]{1,0:T(8,128)(2,1)S(1)} %get-tuple-element.90.own), channel_id=1, source_target_pairs={{0,16},{16,0},{1,17},{17,1},{2,18},{18,2},{3,19},{19,3},{4,20},{20... | collective-permute-start | bytes 1179656 | tf_op jit(solution)/shard_map/ppermute | solution.py:21
  387.1 107.0 %collective-permute-start.81 = (bf16[8,48,3072]{2,1,0:T(8,128)(2,1)}, bf16[8,48,3072]{2,1,0:T(8,128)(2,1)}, u32[]{:S(2)}, u32[]{:S(2)}) collective-permute-start(bf16[8,48,3072]{2,1,0:T(8,128)(2,1)} %dynamic-slice_bitcast_fusion.1), channel_id=1, source_target_pairs={{0,1},{1,0},{2,3},{3,2},{4,5},{5,4},{6,7},{7,6},{8,9},{9,8},{10,11... | collective-permute-start | bytes 7077896 | tf_op jit(solution)/shard_map/ppermute | solution.py:52
  388.8 14.5 %collective-permute-start.73 = (bf16[48,1152]{1,0:T(8,128)(2,1)S(1)}, bf16[48,1152]{1,0:T(8,128)(2,1)S(1)}, u32[]{:S(2)}, u32[]{:S(2)}) collective-permute-start(bf16[48,1152]{1,0:T(8,128)(2,1)S(1)} %fusion.73), channel_id=1, source_target_pairs={{0,4},{1,5},{4,8},{5,9},{8,12},{9,13},{12,14},{13,15},{14,10},{15,... | collective-permute-start | bytes 331784 | tf_op jit(solution)/shard_map/ppermute | solution.py:48
  406.5 20.5 %collective-permute-start.60 = (bf16[256,768]{1,0:T(8,128)(2,1)}, bf16[256,768]{1,0:T(8,128)(2,1)}, u32[]{:S(2)}, u32[]{:S(2)}) collective-permute-start(bf16[256,768]{1,0:T(8,128)(2,1)} %copy-done.114), channel_id=1, source_target_pairs={{0,16},{16,0},{1,17},{17,1},{2,18},{18,2},{3,19},{19,3},{4,20},{20... | collective-permute-start | bytes 1179656 | tf_op jit(solution)/shard_map/ppermute | solution.py:21
  410.7 12.1 %collective-permute-start.77 = (bf16[48,1152]{1,0:T(8,128)(2,1)}, bf16[48,1152]{1,0:T(8,128)(2,1)S(1)}, u32[]{:S(2)}, u32[]{:S(2)}) collective-permute-start(bf16[48,1152]{1,0:T(8,128)(2,1)} %get-tuple-element.169), channel_id=1, source_target_pairs={{0,2},{1,3},{4,0},{5,1},{8,4},{9,5},{12,8},{13,9},{14,12},{15,13},... | collective-permute-start | bytes 331784 | tf_op jit(solution)/shard_map/ppermute | solution.py:48
  427.0 42.1 %collective-permute-start.61 = (bf16[8,48,2048]{2,1,0:T(8,128)(2,1)S(1)}, bf16[8,48,2048]{2,1,0:T(8,128)(2,1)S(1)}, u32[]{:S(2)}, u32[]{:S(2)}) collective-permute-start(bf16[8,48,2048]{2,1,0:T(8,128)(2,1)S(1)} %dynamic-slice_bitcast_fusion.3), channel_id=1, source_target_pairs={{0,1},{1,0},{2,3},{3,2},{4,5},{5,4},{6,7},{7,6},{8,9},{9,8},{10,11... | collective-permute-start | bytes 4718600 | tf_op jit(solution)/shard_map/ppermute | solution.py:52
  429.6 134.4 %collective-permute-start.75 = (bf16[48,1152]{1,0:T(8,128)(2,1)}, bf16[48,1152]{1,0:T(8,128)(2,1)S(1)}, u32[]{:S(2)}, u32[]{:S(2)}) collective-permute-start(bf16[48,1152]{1,0:T(8,128)(2,1)} %get-tuple-element.168), channel_id=1, source_target_pairs={{0,4},{1,5},{4,8},{5,9},{8,12},{9,13},{12,14},{13,15},{14,10},{15,... | collective-permute-start | bytes 331784 | tf_op jit(solution)/shard_map/ppermute | solution.py:48
  433.3 26.8 %collective-permute-start.95 = (bf16[24,3072]{1,0:T(8,128)(2,1)S(1)}, bf16[24,3072]{1,0:T(8,128)(2,1)S(1)}, u32[]{:S(2)}, u32[]{:S(2)}) collective-permute-start(bf16[24,3072]{1,0:T(8,128)(2,1)S(1)} %get-tuple-element.153), channel_id=1, source_target_pairs={{0,2},{1,3},{4,0},{5,1},{8,4},{9,5},{12,8},{13,9},{14,12},{15,13},... | collective-permute-start | bytes 442376 | tf_op jit(solution)/shard_map/ppermute | solution.py:48
  460.1 106.0 %collective-permute-start.79 = (bf16[48,1152]{1,0:T(8,128)(2,1)}, bf16[48,1152]{1,0:T(8,128)(2,1)}, u32[]{:S(2)}, u32[]{:S(2)}) collective-permute-start(bf16[48,1152]{1,0:T(8,128)(2,1)} %fusion.71), channel_id=1, source_target_pairs={{0,2},{1,3},{4,0},{5,1},{8,4},{9,5},{12,8},{13,9},{14,12},{15,13},... | collective-permute-start | bytes 331784 | tf_op jit(solution)/shard_map/ppermute | solution.py:48
  472.3 9.0 %collective-permute-start.96 = (bf16[48,3072]{1,0:T(8,128)(2,1)S(1)}, bf16[48,3072]{1,0:T(8,128)(2,1)S(1)}, u32[]{:S(2)}, u32[]{:S(2)}) collective-permute-start(bf16[48,3072]{1,0:T(8,128)(2,1)S(1)} %get-tuple-element.151), channel_id=1, source_target_pairs={{0,2},{1,3},{4,0},{5,1},{8,4},{9,5},{12,8},{13,9},{14,12},{15,13},... | collective-permute-start | bytes 884744 | tf_op jit(solution)/shard_map/ppermute | solution.py:48
  479.7 112.0 %collective-permute-start.94 = (bf16[48,3072]{1,0:T(8,128)(2,1)}, bf16[48,3072]{1,0:T(8,128)(2,1)S(1)}, u32[]{:S(2)}, u32[]{:S(2)}) collective-permute-start(bf16[48,3072]{1,0:T(8,128)(2,1)} %get-tuple-element.150), channel_id=1, source_target_pairs={{0,4},{1,5},{4,8},{5,9},{8,12},{9,13},{12,14},{13,15},{14,10},{15,... | collective-permute-start | bytes 884744 | tf_op jit(solution)/shard_map/ppermute | solution.py:48
  492.9 10.5 %collective-permute-start.66 = (bf16[24,2048]{1,0:T(8,128)(2,1)S(1)}, bf16[24,2048]{1,0:T(8,128)(2,1)S(1)}, u32[]{:S(2)}, u32[]{:S(2)}) collective-permute-start(bf16[24,2048]{1,0:T(8,128)(2,1)S(1)} %get-tuple-element.167), channel_id=1, source_target_pairs={{0,2},{1,3},{4,0},{5,1},{8,4},{9,5},{12,8},{13,9},{14,12},{15,13},... | collective-permute-start | bytes 294920 | tf_op jit(solution)/shard_map/ppermute | solution.py:48
  503.4 25.8 %collective-permute-start.104 = (bf16[24,4736]{1,0:T(8,128)(2,1)S(1)}, bf16[24,4736]{1,0:T(8,128)(2,1)S(1)}, u32[]{:S(2)}, u32[]{:S(2)}) collective-permute-start(bf16[24,4736]{1,0:T(8,128)(2,1)S(1)} %get-tuple-element.158), channel_id=1, source_target_pairs={{0,4},{1,5},{4,8},{5,9},{8,12},{9,13},{12,14},{13,15},{14,10},{15,... | collective-permute-start | bytes 681992 | tf_op jit(solution)/shard_map/ppermute | solution.py:48
  507.1 9.7 %collective-permute-start.97 = (bf16[48,3072]{1,0:T(8,128)(2,1)S(1)}, bf16[48,3072]{1,0:T(8,128)(2,1)S(1)}, u32[]{:S(2)}, u32[]{:S(2)}) collective-permute-start(bf16[48,3072]{1,0:T(8,128)(2,1)S(1)} %fusion.7), channel_id=1, source_target_pairs={{0,2},{1,3},{4,0},{5,1},{8,4},{9,5},{12,8},{13,9},{14,12},{15,13},... | collective-permute-start | bytes 884744 | tf_op jit(solution)/shard_map/ppermute | solution.py:48
  529.2 28.2 %collective-permute-start.65 = (bf16[48,2048]{1,0:T(8,128)(2,1)S(1)}, bf16[48,2048]{1,0:T(8,128)(2,1)S(1)}, u32[]{:S(2)}, u32[]{:S(2)}) collective-permute-start(bf16[48,2048]{1,0:T(8,128)(2,1)S(1)} %get-tuple-element.164), channel_id=1, source_target_pairs={{0,4},{1,5},{4,8},{5,9},{8,12},{9,13},{12,14},{13,15},{14,10},{15,... | collective-permute-start | bytes 589832 | tf_op jit(solution)/shard_map/ppermute | solution.py:48
  557.4 10.2 %collective-permute-start.86 = (bf16[24,3072]{1,0:T(8,128)(2,1)S(1)}, bf16[24,3072]{1,0:T(8,128)(2,1)S(1)}, u32[]{:S(2)}, u32[]{:S(2)}) collective-permute-start(bf16[24,3072]{1,0:T(8,128)(2,1)S(1)} %get-tuple-element.157), channel_id=1, source_target_pairs={{0,2},{1,3},{4,0},{5,1},{8,4},{9,5},{12,8},{13,9},{14,12},{15,13},... | collective-permute-start | bytes 442376 | tf_op jit(solution)/shard_map/ppermute | solution.py:48
  563.4 28.3 %collective-permute-start.98 = (bf16[48,3072]{1,0:T(8,128)(2,1)S(1)}, bf16[48,3072]{1,0:T(8,128)(2,1)S(1)}, u32[]{:S(2)}, u32[]{:S(2)}) collective-permute-start(bf16[48,3072]{1,0:T(8,128)(2,1)S(1)} %fusion.9), channel_id=1, source_target_pairs={{0,2},{1,3},{4,0},{5,1},{8,4},{9,5},{12,8},{13,9},{14,12},{15,13},... | collective-permute-start | bytes 884744 | tf_op jit(solution)/shard_map/ppermute | solution.py:48
  566.2 16.1 %collective-permute-start.70 = (bf16[48,4]{0,1:T(4,128)(2,1)S(1)}, bf16[48,4]{0,1:T(4,128)(2,1)S(1)}, u32[]{:S(2)}, u32[]{:S(2)}) collective-permute-start(bf16[48,4]{0,1:T(4,128)(2,1)S(1)} %select_convert_fusion.5), channel_id=1, source_target_pairs={{0,16},{16,0},{1,17},{17,1},{2,18},{18,2},{3,19},{19,3},{4,20},{20... | collective-permute-start | bytes 1160 | tf_op jit(solution)/shard_map/ppermute | solution.py:21
  567.6 29.7 %collective-permute-start.80 = (bf16[48,1152]{1,0:T(8,128)(2,1)S(1)}, bf16[48,1152]{1,0:T(8,128)(2,1)S(1)}, u32[]{:S(2)}, u32[]{:S(2)}) collective-permute-start(bf16[48,1152]{1,0:T(8,128)(2,1)S(1)} %get-tuple-element.146), channel_id=1, source_target_pairs={{0,16},{16,0},{1,17},{17,1},{2,18},{18,2},{3,19},{19,3},{4,20},{20... | collective-permute-start | bytes 331784 | tf_op jit(solution)/shard_map/ppermute | solution.py:21
  582.3 9.4 %collective-permute-start.85 = (bf16[48,3072]{1,0:T(8,128)(2,1)S(1)}, bf16[48,3072]{1,0:T(8,128)(2,1)S(1)}, u32[]{:S(2)}, u32[]{:S(2)}) collective-permute-start(bf16[48,3072]{1,0:T(8,128)(2,1)S(1)} %get-tuple-element.154), channel_id=1, source_target_pairs={{0,4},{1,5},{4,8},{5,9},{8,12},{9,13},{12,14},{13,15},{14,10},{15,... | collective-permute-start | bytes 884744 | tf_op jit(solution)/shard_map/ppermute | solution.py:48
  (183 other events, 1771.8 us)
